TPU v7x, 128 devices: a whole 4x4x4 slice. The times are simulated.
128 devices in a mesh: seq: 32 (over y, x, core), head: 4 (over z).
Axes of the slice: x: 4, y: 4, z: 4, core: 2. Of those that a mesh axis runs over, the one named last changes fastest.
Arguments:
- activations: bfloat16 [32768, 2048], P('seq'), may hold values from -1000 to 1000
- w_qk: bfloat16 [2048, 2048], P(None, 'head'), may hold values from -0.125 to 0.125
- w_value: bfloat16 [2048, 2048], P(None, 'head'), may hold values from -0.125 to 0.125
- w_out: bfloat16 [2048, 2048], P('head'), may hold values from -0.125 to 0.125
- bucket_order: int32 [2, 16, 32768], P(None, 'head', 'seq'), may hold values from 0 to 1023, as said below
- span_sends: int32 [2, 16, 32, 32], P(None, 'head'), may hold values from 0 to 2, as said below
Outputs:
- attended: bfloat16 [32768, 2048], P('seq', 'head')
Inputs may be any that keep to these rules, and one draw needn't show every extreme that they name: `bucket_order`: each aligned block of 1024 entries along the last dimension is a permutation of 0 to 1023. span_sends[r, h, s, j] counts the spans of block s that go to bucket range j; for each r, h, s the counts sum to 16. In every round and head one bucket range receives 2 from every block, and every bucket range receives at least one span.
All inputs are finite; a program needn't handle non-finite values.
Results may differ from a plain program's by a relative error of at most 0.015.
The roundings to bfloat16 on the way count: a program that leaves them out, or rounds other values in their place, can miss the bound.
Values may be sent and summed in bfloat16 or wider, within the bound.
No kernel may reach another device: no remote copies, remote signals or barrier semaphores. Data moves between devices by JAX's collectives and lax.ppermute only.
A program may use at most 192 MiB of HBM per device.

v0:
```python
import math

import jax
import jax.numpy as jnp
from jax import lax
from jax.sharding import PartitionSpec as P

HEAD_DIM = 128
SPAN = 64


EPS = 1e-06
SELF_SCORE = -100000.0


def passed_along(shard, axis, by):
    devices = lax.axis_size(axis)
    return lax.ppermute(shard, axis, [(i, (i + by) % devices) for i in range(devices)])


def take_rows(source, indices):
    return jax.vmap(lambda blocks, positions: blocks[positions])(source, indices)


def slot_index(counts, slot_cap):
    starts = jnp.cumsum(counts, axis=-1) - counts
    offsets = jnp.arange(slot_cap, dtype=jnp.int32)
    indices = starts[:, :, None] + offsets[None, None, :]
    filled = offsets[None, None, :] < counts[:, :, None]
    return (indices, filled)


def locate(counts, slot_cap, length):
    inclusive = jnp.cumsum(counts, axis=-1)
    starts = inclusive - counts
    places = jnp.arange(length, dtype=jnp.int32)
    owners = jnp.sum((inclusive[:, None, :] <= places[None, :, None]).astype(jnp.int32), axis=-1)
    owners = jnp.minimum(owners, counts.shape[1] - 1)
    offset = places[None, :] - jnp.take_along_axis(starts, owners, axis=1)
    offset = jnp.clip(offset, 0, slot_cap - 1)
    return (owners * slot_cap + offset, inclusive[:, -1])


def attend(spans, send_counts, recv_counts, slot_cap):
    groups = spans.shape[0]
    span_count = spans.shape[1]
    seq_count = send_counts.shape[1]
    row_width = spans.shape[-1]
    slot_total = seq_count * slot_cap
    indices, filled = slot_index(send_counts, slot_cap)
    picked = take_rows(spans, jnp.clip(indices, 0, span_count - 1).reshape(groups, -1))
    picked = picked.reshape(groups, seq_count, slot_cap, SPAN, row_width)
    outgoing = jnp.where(filled[:, :, :, None, None], picked, jnp.zeros_like(picked))
    arrived = lax.all_to_all(outgoing, "seq", split_axis=1, concat_axis=1, tiled=True)
    flat_index, totals = locate(recv_counts, slot_cap, slot_total)
    stream = take_rows(arrived.reshape(groups, slot_total, SPAN, row_width), flat_index)
    last_index = jnp.maximum(totals - 1, 0)
    last_rows = jnp.take_along_axis(stream, last_index[:, None, None, None], axis=1)
    before = passed_along(last_rows, "seq", 1)
    left_rows = jnp.concatenate([before, stream[:, :-1]], axis=1)
    key_rows = jnp.concatenate([left_rows, stream], axis=2)
    queries = stream[..., :HEAD_DIM]
    key_part = key_rows[..., :HEAD_DIM]
    value_part = key_rows[..., HEAD_DIM:]
    scores = jnp.einsum("gpqe,gpke->gpqk", queries, key_part, preferred_element_type=jnp.float32)
    squares = jnp.einsum("gpke,gpke->gpk", key_part, key_part, preferred_element_type=jnp.float32)
    scaling = lax.rsqrt(squares + EPS) * (1.0 / math.sqrt(HEAD_DIM))
    scores = scores * scaling[:, :, None, :]
    query_at = jnp.arange(SPAN, dtype=jnp.int32)[:, None]
    key_at = jnp.arange(2 * SPAN, dtype=jnp.int32)[None, :]
    scores = jnp.where((key_at == query_at + SPAN)[None, None], jnp.float32(SELF_SCORE), scores)
    summit = jnp.max(scores, axis=-1, keepdims=True)
    raised = jnp.exp(scores - summit)
    sums_row = jnp.sum(raised, axis=-1, keepdims=True)
    weights = (raised / sums_row).astype(jnp.bfloat16)
    mixed = jnp.einsum(
        "gpqk,gpke->gpqe", weights, value_part, preferred_element_type=jnp.float32
    ).astype(jnp.bfloat16)
    log_total = (summit + jnp.log(sums_row))[..., 0]
    back_index, back_filled = slot_index(recv_counts, slot_cap)
    back_flat = jnp.clip(back_index, 0, slot_total - 1).reshape(groups, -1)
    back_rows = take_rows(mixed, back_flat).reshape(groups, seq_count, slot_cap, SPAN, HEAD_DIM)
    back_lse = take_rows(log_total, back_flat).reshape(groups, seq_count, slot_cap, SPAN)
    keep_slot = back_filled[:, :, :, None]
    back_rows = jnp.where(keep_slot[..., None], back_rows, jnp.zeros_like(back_rows))
    back_lse = jnp.where(keep_slot, back_lse, jnp.zeros_like(back_lse))
    home_rows, home_lse = (
        lax.all_to_all(
            back_rows.astype(jnp.float32), "seq", split_axis=1, concat_axis=1, tiled=True
        ).astype(back_rows.dtype),
        lax.all_to_all(back_lse, "seq", split_axis=1, concat_axis=1, tiled=True),
    )
    home_index, home_total = locate(send_counts, slot_cap, span_count)
    rows_out = take_rows(home_rows.reshape(groups, slot_total, SPAN, HEAD_DIM), home_index)
    lse_out = take_rows(home_lse.reshape(groups, slot_total, SPAN), home_index)
    return (rows_out, lse_out)


def body(activations, w_qk, w_value, w_out, bucket_order, span_sends):
    seq_count = lax.axis_size("seq")
    my_index = lax.axis_index("seq")
    tok_rows = activations.shape[0]
    head_local = w_qk.shape[1] // HEAD_DIM
    round_count = bucket_order.shape[0]
    span_count = tok_rows // SPAN
    slot_cap = max(2, 2 * span_count // seq_count)
    keyed = jnp.dot(activations, w_qk, preferred_element_type=jnp.float32).astype(jnp.bfloat16)
    valued = jnp.dot(activations, w_value, preferred_element_type=jnp.float32).astype(jnp.bfloat16)
    keyed = keyed.reshape(tok_rows, head_local, HEAD_DIM)
    valued = valued.reshape(tok_rows, head_local, HEAD_DIM)
    paired = jnp.transpose(jnp.concatenate([keyed, valued], axis=-1), (1, 0, 2))
    sorted_rows = jax.vmap(lambda positions: take_rows(paired, positions))(bucket_order)
    sorted_rows = sorted_rows.reshape(round_count, head_local, span_count, SPAN, 2 * HEAD_DIM)
    send_counts = jnp.take(span_sends, my_index, axis=2)
    recv_counts = jnp.take(span_sends, my_index, axis=3)
    results = [
        attend(sorted_rows[round_at], send_counts[round_at], recv_counts[round_at], slot_cap)
        for round_at in range(round_count)
    ]
    rows_out = jnp.concatenate([result_pair[0] for result_pair in results], axis=0)
    lse_out = jnp.concatenate([result_pair[1] for result_pair in results], axis=0)
    rows_out = rows_out.reshape(round_count, head_local, tok_rows, HEAD_DIM)
    lse_out = lse_out.reshape(round_count, head_local, tok_rows)
    counting = jnp.arange(tok_rows, dtype=jnp.int32)
    inverse = jax.vmap(
        lambda positions: jnp.zeros((tok_rows,), jnp.int32).at[positions].set(counting)
    )(bucket_order.reshape(-1, tok_rows))
    inverse = inverse.reshape(round_count, head_local, tok_rows)
    token_rows = jax.vmap(take_rows)(rows_out, inverse)
    token_lse = jax.vmap(take_rows)(lse_out, inverse)
    round_peak = jnp.max(token_lse, axis=0, keepdims=True)
    shares = jnp.exp(token_lse - round_peak)
    shares = shares / jnp.sum(shares, axis=0, keepdims=True)
    blended = jnp.sum(shares[..., None] * token_rows.astype(jnp.float32), axis=0)
    combined = (
        jnp.transpose(blended, (1, 0, 2))
        .reshape(tok_rows, head_local * HEAD_DIM)
        .astype(jnp.bfloat16)
    )
    partial_value = jnp.dot(combined, w_out, preferred_element_type=jnp.float32)
    return lax.psum_scatter(
        partial_value.astype(jnp.bfloat16), "head", scatter_dimension=1, tiled=True
    )


def solution(mesh):
    in_specs = (
        P("seq", None),
        P(None, "head"),
        P(None, "head"),
        P("head", None),
        P(None, "head", "seq"),
        P(None, "head", None, None),
    )
    out_specs = P("seq", "head")
    return jax.shard_map(body, mesh=mesh, in_specs=in_specs, out_specs=out_specs, check_vma=False)
```

profile of v0, /device:TPU:0, one launch (start us, length us, event | category | flops | bytes accessed | tf_op | source)
XLA Modules:
  0.0 990.0 jit_solution(12889758160194296376)
XLA Ops:
  29.8 136.2 %gather_fusion = bf16[8192,256]{1,0:T(8,128)(2,1)} fusion(bf16[4,1024,256]{2,1,0:T(8,128)(2,1)} %maximum_bitcast_fusion, s32[8192]{0:T(1024)S(1)} %bitcast.173), kind=kCustom, calls=%fused_computation.6 | custom fusion | bytes 8454144 | tf_op jit(solution)/shard_map/vmap(vmap())/gather | solution.py:22
  170.7 11.7 %gather_fusion.1 = bf16[256,64,256]{2,1,0:T(8,128)(2,1)} fusion(bf16[4,16,64,256]{3,2,1,0:T(8,128)(2,1)} %bitcast.184, s32[256]{0:T(256)S(1)} %reshape.657), kind=kCustom, calls=%fused_computation.7 | custom fusion | bytes 16779264 | tf_op jit(solution)/shard_map/vmap()/gather | solution.py:22
  189.7 8.3 copy.108
  205.9 11.7 %gather_fusion.5 = bf16[256,64,256]{2,1,0:T(8,128)(2,1)} fusion(bf16[4,16,64,256]{3,2,1,0:T(8,128)(2,1)} %bitcast.183, s32[256]{0:T(256)S(1)} %reshape.681), kind=kCustom, calls=%fused_computation.11 | custom fusion | bytes 16779264 | tf_op jit(solution)/shard_map/vmap()/gather | solution.py:22
  224.8 8.3 copy.117
  233.0 78.6 %all-to-all-done = bf16[4,32,2,64,256]{4,3,2,0,1:T(8,128)(2,1)} async-done(((bf16[4,32,2,64,256]{4,3,2,0,1:T(8,128)(2,1)}), bf16[4,32,2,64,256]{4,3,2,0,1:T(8,128)(2,1)}, u32[]{:S(2)}, u32[]{:S(2)}) %all-to-all-start) | async-done | bytes 8388640 | tf_op jit(solution)/shard_map/all_to_all | solution.py:54
  323.3 8.3 copy.109
  331.6 13.4 %gather_fusion.2 = bf16[256,64,256]{2,1,0:T(8,128)(2,1)} fusion(bf16[4,64,64,256]{3,2,1,0:T(8,128)(2,1)} %bitcast.187, s32[256]{0:T(256)S(1)} %reshape.663), kind=kCustom, calls=%fused_computation.8 | custom fusion | bytes 16779264 | tf_op jit(solution)/shard_map/vmap()/gather | solution.py:22
  345.0 8.1 slice.146
  357.4 65.1 %all-to-all-done.2 = bf16[4,32,2,64,256]{4,3,2,0,1:T(8,128)(2,1)} async-done(((bf16[4,32,2,64,256]{4,3,2,0,1:T(8,128)(2,1)}), bf16[4,32,2,64,256]{4,3,2,0,1:T(8,128)(2,1)}, u32[]{:S(2)}, u32[]{:S(2)}) %all-to-all-start.2) | async-done | bytes 8388640 | tf_op jit(solution)/shard_map/all_to_all | solution.py:54
  422.5 8.3 copy.118
  430.7 13.4 %gather_fusion.6 = bf16[256,64,256]{2,1,0:T(8,128)(2,1)} fusion(bf16[4,64,64,256]{3,2,1,0:T(8,128)(2,1)} %bitcast.188, s32[256]{0:T(256)S(1)} %reshape.687), kind=kCustom, calls=%fused_computation.12 | custom fusion | bytes 16779264 | tf_op jit(solution)/shard_map/vmap()/gather | solution.py:22
  444.2 8.1 slice.152
  456.4 13.9 %pad_maximum_fusion = bf16[4,64,128,256]{3,2,1,0:T(8,128)(2,1)} fusion(bf16[4,64,64,256]{3,2,1,0:T(8,128)(2,1)} %bitcast.177, bf16[4,63,64,256]{3,2,1,0:T(8,128)(2,1)} %slice.146, bf16[4,1,64,256]{3,2,1,0:T(8,128)(2,1)S(1)} %collective-permute-done), kind=kLoop, calls=%fused_computation.22 | loop fusion | flops 50331648 | bytes 33554432 | tf_op jit(solution)/shard_map/concatenate | solution.py:61
  478.1 14.0 %pad_maximum_fusion.1 = bf16[4,64,128,256]{3,2,1,0:T(8,128)(2,1)} fusion(bf16[4,64,64,256]{3,2,1,0:T(8,128)(2,1)} %bitcast.181, bf16[4,63,64,256]{3,2,1,0:T(8,128)(2,1)} %slice.152, bf16[4,1,64,256]{3,2,1,0:T(8,128)(2,1)S(1)} %collective-permute-done.1), kind=kLoop, calls=%fused_computation.23 | loop fusion | flops 50331648 | bytes 33554432 | tf_op jit(solution)/shard_map/concatenate | solution.py:61
  500.0 13.8 %fusion.6 = (f32[4,64,64]{2,1,0:T(8,128)S(1)}, f32[4,64,64,128]{3,2,1,0:T(8,128)}) fusion(f32[4,64,128]{2,1,0:T(8,128)S(1)} %rsqrt_multiply_fusion.1, pred[64,128]{1,0:T(8,128)(4,1)S(1)} %iota_compare_fusion.8, bf16[4,64,128,256]{3,2,1,0:T(8,128)(2,1)} %pad_maximum_fusion, bf16[4,64,64,256]{3,2,1,0:T(8,128)(2,1)} %bitcast.178), kind=kOutput, calls=%fused_computation.42 | convolution fusion | flops 543145984 | bytes 21176320 | tf_op jit(solution)/shard_map/gpqe,gpke->gpqk/dot_general | solution.py:65
  513.8 13.4 %fusion.12 = (f32[4,64,64]{2,1,0:T(8,128)S(1)}, f32[4,64,64]{2,1,0:T(8,128)S(1)}, f32[4,64,64,128]{3,2,1,0:T(8,128)}) fusion(f32[4,64,64,128]{3,2,1,0:T(8,128)} %get-tuple-element.49, f32[4,64,64]{2,1,0:T(8,128)S(1)} %get-tuple-element.48, f32[4,64,128]{2,1,0:T(8,128)S(1)} %rsqrt_multiply_fusion.1, pred[64,128]{1,0:T(8,128)(4,1)S(1)} %iota_compare_fusion.8, ...), kind=kOutput, calls=%fused_computation.48 | convolution fusion | flops 551518208 | bytes 29827072 | tf_op jit(solution)/shard_map/gpqe,gpke->gpqk/dot_general | solution.py:65
  527.3 10.4 %fusion.29 = bf16[4,64,64,128]{3,2,1,0:T(8,128)(2,1)} fusion(bf16[4,64,128,256]{3,2,1,0:T(8,128)(2,1)} %pad_maximum_fusion, f32[4,64,64,128]{3,2,1,0:T(8,128)} %get-tuple-element.49, f32[4,64,64]{2,1,0:T(8,128)S(1)} %get-tuple-element.30, f32[4,64,64]{2,1,0:T(8,128)S(1)} %get-tuple-element.48, f32[4,64,128]{2,1,0:T(8,128)S(1)} %rsqrt_multiply_fusion.1, ...), kind=kOutput, calls=%fused_computation.69 | convolution fusion | flops 549453824 | bytes 21241856 | tf_op jit(solution)/shard_map/gpqk,gpke->gpqe/dot_general | solution.py:76
  582.2 10.2 %fusion.32 = bf16[4,64,64,128]{3,2,1,0:T(8,128)(2,1)} fusion(bf16[4,64,128,256]{3,2,1,0:T(8,128)(2,1)} %pad_maximum_fusion.1, f32[4,64,64,128]{3,2,1,0:T(8,128)} %get-tuple-element.50, f32[4,64,64]{2,1,0:T(8,128)S(1)} %fusion.13, f32[4,64,64]{2,1,0:T(8,128)S(1)} %get-tuple-element.31, f32[4,64,128]{2,1,0:T(8,128)S(1)} %rsqrt_multiply_fusion, ...), kind=kOutput, calls=%fused_computation.70 | convolution fusion | flops 549453824 | bytes 21241856 | tf_op jit(solution)/shard_map/gpqk,gpke->gpqe/dot_general | solution.py:76
  601.7 34.0 %all-to-all-done.4 = bf16[4,32,2,64,128]{4,3,2,0,1:T(8,128)(2,1)} async-done(((bf16[4,32,2,64,128]{4,3,2,0,1:T(8,128)(2,1)}), bf16[4,32,2,64,128]{4,3,2,0,1:T(8,128)(2,1)}, u32[]{:S(2)}, u32[]{:S(2)}) %all-to-all-start.4) | async-done | bytes 4194336 | tf_op jit(solution)/shard_map/all_to_all | solution.py:88
  643.8 30.5 %scatter_custom_fusion = s32[8192]{0:T(1024)S(1)} fusion(s32[8192]{0:T(1024)S(1)} %get-tuple-element.58, s32[8192]{0:T(1024)S(1)} %get-tuple-element.57, s32[]{:T(128)} %constant.33.clone.1), kind=kCustom, calls=%fused_computation.122 | custom fusion | bytes 32772
  678.8 80.1 %gather_fusion.9 = f32[8192]{0:T(1024)S(1)} fusion(f32[2,4,1024]{2,1,0:T(4,128)S(1)} %reshape.518, s32[8192]{0:T(1024)S(1)} %bitcast.171), kind=kCustom, calls=%fused_computation.15 | custom fusion | bytes 163840 | tf_op jit(solution)/shard_map/vmap(vmap())/gather | solution.py:22
  780.6 143.0 %gather_fusion.14 = bf16[8192,128]{1,0:T(8,128)(2,1)} fusion(bf16[2,4,1024,128]{3,2,1,0:T(8,128)(2,1)} %bitcast.174, s32[8192]{0:T(1024)S(1)} %bitcast.172), kind=kCustom, calls=%fused_computation.20 | custom fusion | bytes 4292608 | tf_op jit(solution)/shard_map/vmap(vmap())/gather | solution.py:22
  933.2 49.5 %reduce-scatter.2.cloned.1.call-done = bf16[1024,512]{1,0:T(8,128)(2,1)} async-done(((bf16[1024,2048]{1,0:T(8,128)(2,1)}), bf16[1024,512]{1,0:T(8,128)(2,1)}) %reduce-scatter.2.cloned.1.call-update) | async-done | bytes 1048592 | tf_op jit(solution)/shard_map/reduce_scatter | solution.py:141
  (180 shorter events, 183.3 us)
Async XLA Ops:
  6.5 921.1 %copy-start = (bf16[512,2048]{1,0:T(8,128)(2,1)S(1)}, bf16[512,2048]{1,0:T(8,128)(2,1)}, u32[]{:S(2)}) copy-start(bf16[512,2048]{1,0:T(8,128)(2,1)} %param.15) | copy-start | bytes 6291460
  8.9 8.0 copy-start.9
  9.1 0.9 copy-start.7
  10.0 6.8 copy-start.1
  10.0 6.8 copy-start.3
  18.5 8.5 copy-start.5
  197.9 113.7 %all-to-all-start = ((bf16[4,32,2,64,256]{4,3,2,0,1:T(8,128)(2,1)}), bf16[4,32,2,64,256]{4,3,2,0,1:T(8,128)(2,1)}, u32[]{:S(2)}, u32[]{:S(2)}) async-start(bf16[4,32,2,64,256]{4,3,2,0,1:T(8,128)(2,1)} %copy.108), calls=%async_computation | async-start | bytes 16777216 | tf_op jit(solution)/shard_map/all_to_all | solution.py:54
  311.6 110.8 %all-to-all-start.2 = ((bf16[4,32,2,64,256]{4,3,2,0,1:T(8,128)(2,1)}), bf16[4,32,2,64,256]{4,3,2,0,1:T(8,128)(2,1)}, u32[]{:S(2)}, u32[]{:S(2)}) async-start(bf16[4,32,2,64,256]{4,3,2,0,1:T(8,128)(2,1)} %copy.117), calls=%async_computation.2 | async-start | bytes 16777216 | tf_op jit(solution)/shard_map/all_to_all | solution.py:54
  357.2 99.2 %collective-permute-start = (bf16[4,1,64,256]{3,2,1,0:T(8,128)(2,1)S(1)}, bf16[4,1,64,256]{3,2,1,0:T(8,128)(2,1)S(1)}, u32[]{:S(2)}, u32[]{:S(2)}) collective-permute-start(bf16[4,1,64,256]{3,2,1,0:T(8,128)(2,1)S(1)} %bitcast_select_fusion.1), channel_id=1, source_target_pairs={{0,4},{4,8},{8,12},{12,16},{16,20},{20,24},{24,28},{28,32},{32,36}... | collective-permute-start | bytes 393224 | tf_op jit(solution)/shard_map/ppermute | solution.py:18
  456.3 21.8 %collective-permute-start.1 = (bf16[4,1,64,256]{3,2,1,0:T(8,128)(2,1)S(1)}, bf16[4,1,64,256]{3,2,1,0:T(8,128)(2,1)S(1)}, u32[]{:S(2)}, u32[]{:S(2)}) collective-permute-start(bf16[4,1,64,256]{3,2,1,0:T(8,128)(2,1)S(1)} %bitcast_select_fusion), channel_id=1, source_target_pairs={{0,4},{4,8},{8,12},{12,16},{16,20},{20,24},{24,28},{28,32},{32,36}... | collective-permute-start | bytes 393224 | tf_op jit(solution)/shard_map/ppermute | solution.py:18
  540.5 22.0 %all-to-all-start.1 = ((f32[32,1,512]{2,1,0:T(1,128)}), f32[32,1,512]{2,1,0:T(1,128)S(1)}, u32[]{:S(2)}, u32[]{:S(2)}) async-start(f32[32,1,512]{2,1,0:T(1,128)} %reshape.846), calls=%async_computation.1 | async-start | bytes 131072 | tf_op jit(solution)/shard_map/all_to_all | solution.py:91
  562.5 14.9 %all-to-all-start.3 = ((f32[32,1,512]{2,1,0:T(1,128)}), f32[32,1,512]{2,1,0:T(1,128)S(1)}, u32[]{:S(2)}, u32[]{:S(2)}) async-start(f32[32,1,512]{2,1,0:T(1,128)} %reshape.844), calls=%async_computation.3 | async-start | bytes 131072 | tf_op jit(solution)/shard_map/all_to_all | solution.py:91
  577.4 58.3 %all-to-all-start.4 = ((bf16[4,32,2,64,128]{4,3,2,0,1:T(8,128)(2,1)}), bf16[4,32,2,64,128]{4,3,2,0,1:T(8,128)(2,1)}, u32[]{:S(2)}, u32[]{:S(2)}) async-start(bf16[4,32,2,64,128]{4,3,2,0,1:T(8,128)(2,1)} %fusion.18), calls=%async_computation.4 | async-start | bytes 8388608 | tf_op jit(solution)/shard_map/all_to_all | solution.py:88
  601.7 39.2 %copy-start.6 = (s32[2,4,1024]{2,1,0:T(4,128)S(1)}, s32[2,4,1024]{2,1,0:T(4,128)}, u32[]{:S(2)}) copy-start(s32[2,4,1024]{2,1,0:T(4,128)} %param.16) | copy-start | bytes 98308
  601.7 39.2 %copy-start.10 = (s32[4,32]{1,0:T(4,128)S(1)}, s32[4,32]{1,0:T(4,128)}, u32[]{:S(2)}) copy-start(s32[4,32]{1,0:T(4,128)} %copy-done.9) | copy-start | bytes 1540
  601.7 39.5 %copy-start.4 = (s32[4,32]{1,0:T(4,128)S(1)}, s32[4,32]{1,0:T(4,128)}, u32[]{:S(2)}) copy-start(s32[4,32]{1,0:T(4,128)} %copy-done.3) | copy-start | bytes 1540
  601.7 40.6 %copy-start.8 = (s32[4,32]{1,0:T(4,128)S(1)}, s32[4,32]{1,0:T(4,128)}, u32[]{:S(2)}) copy-start(s32[4,32]{1,0:T(4,128)} %copy-done.7) | copy-start | bytes 1540
  601.7 40.8 %copy-start.2 = (s32[4,32]{1,0:T(4,128)S(1)}, s32[4,32]{1,0:T(4,128)}, u32[]{:S(2)}) copy-start(s32[4,32]{1,0:T(4,128)} %copy-done.1) | copy-start | bytes 1540
  635.7 132.3 %all-to-all-start.5 = ((bf16[4,32,2,64,128]{4,3,2,0,1:T(8,128)(2,1)}), bf16[4,32,2,64,128]{4,3,2,0,1:T(8,128)(2,1)}, u32[]{:S(2)}, u32[]{:S(2)}) async-start(bf16[4,32,2,64,128]{4,3,2,0,1:T(8,128)(2,1)} %fusion.17), calls=%async_computation.5 | async-start | bytes 8388608 | tf_op jit(solution)/shard_map/all_to_all | solution.py:88
  640.6 3.1 copy-start.12
  640.6 3.1 copy-start.11
  640.6 342.1 %reduce-scatter.2.cloned.1.call-start = ((), (), s32[]{:S(2)}) async-start(), calls=%async_computation.7 | async-start | bytes 5242880 | tf_op jit(solution)/shard_map/reduce_scatter | solution.py:141
Sparse Core Ops, SparseCore 0:
  933.3 49.3 reduce-scatter.1
where the time goes:
time: 1000 us; the launch traced here: 990 us
  local copies, waits for them, and re-layouts  554 us (55%)
  waiting for transfers between devices  231 us (23%)
  other arithmetic  87.6 us (9%)
  matrix products  65.7 us (7%)
  starting transfers between devices  37.1 us (4%)
  between operations  14.5 us (1%)
    gather x24, local copies, waits for them, and re-layouts, take_rows(): blocks[positions]  434 us
    all_to_all x2, waiting for transfers between devices, attend(): lax.all_to_all(outgoing, 'seq', split_axis=1, concat_axis=1, tiled=True)  144 us
    reduce_scatter x1, waiting for transfers between devices, body(): lax.psum_scatter(partial_value.astype(jnp.bfloat16), 'head', scatter_dime...  49.5 us
    all_to_all x2, waiting for transfers between devices, attend(): lax.all_to_all(back_rows.astype(jnp.float32), 'seq', split_axis=1, concat...  34 us
    unnamed x37, local copies, waits for them, and re-layouts  32.4 us
    concatenate x2, other arithmetic, attend(): key_rows = jnp.concatenate([left_rows, stream], axis=2)  28 us
    dot_general x2, matrix products, attend(): jnp.einsum('gpqe,gpke->gpqk', queries, key_part, preferred_element_type=j...  27.2 us
    dot_general x2, matrix products, attend(): jnp.einsum('gpqk,gpke->gpqe', weights, value_part, preferred_element_type...  20.6 us
  transfers between devices with their start and end apart: 9, of which 5 were waited for; matrix products, arithmetic and copies ran while one was open for 29% of the time, Pallas kernels for 0%

commit v1 on v0

v1 whole, which is shorter than its diff:
```python
import functools
import math

import jax
import jax.numpy as jnp
from jax import lax
from jax.experimental import pallas as pl
from jax.experimental.pallas import tpu as pltpu
from jax.sharding import PartitionSpec as P

HEAD_DIM = 128
SPAN = 64
EPS = 1e-06
SELF_SCORE = -100000.0
QUARTER = 16
QUARTERS = SPAN // QUARTER
PAIR = 2
SENT = 15
VMEM_LIMIT = 63 * 1024 * 1024


def params(**kwargs):
    return pltpu.CompilerParams(vmem_limit_bytes=VMEM_LIMIT, **kwargs)


def spare_span(sends_ref, r, head, me):
    counts = sends_ref[r, head, pl.ds(me, 1), :].astype(jnp.float32)
    at = lax.broadcasted_iota(jnp.int32, counts.shape, 1).astype(jnp.float32)
    first = jnp.min(jnp.where(counts > 1.5, at, float(counts.shape[1])))
    before = jnp.sum(jnp.where(at < first, counts, 0.0))
    return jnp.clip(before.astype(jnp.int32), 0, SENT - 1)


def sort_kernel(
    me_ref, sends_ref, act_ref, wq_ref, wv_ref, order_ref, out_ref, sent_ref, kv_ref, onehot_ref
):
    tokens = act_ref.shape[0]
    spans = tokens // SPAN
    rounds = out_ref.shape[0]
    head = pl.program_id(0)
    lanes = 128
    token_at = lax.broadcasted_iota(jnp.int32, (lanes, tokens), 1).astype(jnp.float32)
    for r in range(rounds):
        row = order_ref[r, pl.ds(head, 1), :].astype(jnp.float32)
        parts = [row[:, j : j + lanes] for j in range(0, tokens, lanes)]
        wanted = jnp.concatenate(parts, axis=0).T
        for j in range(tokens // lanes):
            onehot = jnp.where(wanted[:, j : j + 1] == token_at, 1.0, 0.0)
            onehot_ref[r, j * lanes : (j + 1) * lanes, :] = onehot.astype(jnp.bfloat16)
    weights = jnp.concatenate([wq_ref[...], wv_ref[...]], axis=1)
    kv_ref[...] = jnp.dot(
        act_ref[...], weights, preferred_element_type=jnp.float32
    ).astype(jnp.bfloat16)

    def one_round(r, carry):
        rows = jnp.dot(onehot_ref[r], kv_ref[...], preferred_element_type=jnp.float32)
        rows = rows.astype(jnp.bfloat16)
        for at in range(2):
            half = rows[:, at * HEAD_DIM : (at + 1) * HEAD_DIM]
            half = half.reshape(spans, QUARTERS, QUARTER, HEAD_DIM)
            for quarter in range(QUARTERS):
                out_ref[r, 0, at, quarter, 0] = half[:, quarter]
        spare = spare_span(sends_ref, r, head, me_ref[0])
        for at in range(2):
            tiles = [
                out_ref[r, 0, at, :, 0, j + (j >= spare).astype(jnp.int32)] for j in range(SENT)
            ]
            for j, tile in enumerate(tiles):
                sent_ref[r, 0, at, :, 0, j] = tile
        return carry

    lax.fori_loop(0, rounds, one_round, 0)


def project_and_sort(me, sends, activations, w_qk, w_value, order):
    tokens, width = activations.shape
    rounds, heads = order.shape[:2]
    block = (rounds, 1, 2, QUARTERS, 1, tokens // SPAN, QUARTER, HEAD_DIM)
    shape = (rounds, PAIR, 2, QUARTERS, heads // PAIR) + block[5:]
    return pl.pallas_call(
        sort_kernel,
        grid=(heads,),
        in_specs=[
            pl.BlockSpec(memory_space=pltpu.SMEM),
            pl.BlockSpec(sends.shape, lambda h: (0, 0, 0, 0)),
            pl.BlockSpec((tokens, width), lambda h: (0, 0)),
            pl.BlockSpec((width, HEAD_DIM), lambda h: (0, h)),
            pl.BlockSpec((width, HEAD_DIM), lambda h: (0, h)),
            pl.BlockSpec(order.shape, lambda h: (0, 0, 0)),
        ],
        out_specs=[
            pl.BlockSpec(block, lambda h: (0, h % PAIR, 0, 0, h // PAIR, 0, 0, 0)),
            pl.BlockSpec(
                block[:5] + (SENT,) + block[6:],
                lambda h: (0, h % PAIR, 0, 0, h // PAIR, 0, 0, 0),
            ),
        ],
        out_shape=[
            jax.ShapeDtypeStruct(shape, jnp.bfloat16),
            jax.ShapeDtypeStruct(shape[:5] + (SENT,) + shape[6:], jnp.bfloat16),
        ],
        scratch_shapes=[
            pltpu.VMEM((tokens, 2 * HEAD_DIM), jnp.bfloat16),
            pltpu.VMEM((rounds, tokens, tokens), jnp.bfloat16),
        ],
        compiler_params=params(),
        cost_estimate=pl.CostEstimate(
            flops=heads * tokens * 4 * HEAD_DIM * (width + rounds * tokens),
            bytes_accessed=2 * tokens * width + heads * 4 * HEAD_DIM * (width + 2 * tokens),
            transcendentals=0,
        ),
    )(me, sends, activations, w_qk, w_value, order)


def left_table(counts):
    blocks, ranges = counts.shape[1:]
    spans = SENT + 1
    at = jnp.arange(ranges, dtype=jnp.int32)
    block_at = jnp.arange(blocks, dtype=jnp.int32)
    upto = at[:, None] <= at[None, :]
    inclusive = jnp.sum(jnp.where(upto[None, None], counts[:, :, :, None], 0), axis=2)
    exclusive = inclusive - counts
    spare = jnp.min(jnp.where(counts > 1, exclusive, SENT - 1), axis=2)[:, :, None]
    ends = inclusive - 1
    ends = block_at[None, :, None] * spans + ends - (ends > spare).astype(jnp.int32)
    tails = jnp.where(counts > 0, ends, -1)
    earlier = block_at[:, None] < block_at[None, :]
    before = jnp.max(
        jnp.where(earlier[None, :, :, None], tails[:, :, None, :], -1), axis=1
    )
    last = jnp.max(tails, axis=1)
    wrapped = jnp.roll(last, 1, axis=-1)
    before = jnp.where(before < 0, wrapped[:, None, :], before)
    k_at = jnp.arange(SENT, dtype=jnp.int32)[None, None, :]
    k_at = k_at + (k_at > spare).astype(jnp.int32)
    here = k_at - 1
    here = block_at[None, :, None] * spans + here - (here > spare).astype(jnp.int32)
    k_at, here = k_at[..., None], here[..., None]
    first = exclusive[:, :, None, :]
    mine = (first <= k_at) & (k_at < inclusive[:, :, None, :])
    left = jnp.where(k_at > first, here, before[:, :, None, :])
    left = jnp.sum(jnp.where(mine, left, 0), axis=-1)
    return jnp.clip(left, 0, blocks * spans - 2).reshape(counts.shape[0], blocks * SENT)


def permute_kernel(pair, table_ref, in_ref, out_ref):
    steps, sent = out_ref.shape[:2]
    start = pl.program_id(0) * steps

    def one_block(t, carry):
        tiles = []
        for k in range(sent):
            place = table_ref[pair, (start + t) * sent + k]
            tiles.append(in_ref[place >> 4, 0, place & 15])
        for k, tile in enumerate(tiles):
            out_ref[t, k] = tile
        return carry

    lax.fori_loop(0, steps, one_block, 0)


def permute(table, pieces, pair):
    blocks, _, sent, rows, columns = pieces.shape
    steps = 4
    size = blocks * sent * rows * columns
    return pl.pallas_call(
        functools.partial(permute_kernel, pair),
        grid=(steps,),
        in_specs=[
            pl.BlockSpec(memory_space=pltpu.SMEM),
            pl.BlockSpec((blocks, 1, sent, rows, columns), lambda i: (0, pair, 0, 0, 0)),
        ],
        out_specs=pl.BlockSpec((blocks // steps, sent, rows, columns), lambda i: (i, 0, 0, 0)),
        out_shape=jax.ShapeDtypeStruct((blocks, sent, rows, columns), jnp.bfloat16),
        compiler_params=params(),
        cost_estimate=pl.CostEstimate(flops=size, bytes_accessed=4 * size, transcendentals=0),
    )(table, pieces)


def as_spans(quarters):
    spans = quarters.shape[1]
    return jnp.swapaxes(quarters, 0, 1).reshape(spans, SPAN, HEAD_DIM)


def batched(left, right, left_dim, right_dim):
    return lax.dot_general(
        left,
        right,
        (((left_dim,), (right_dim,)), ((0,), (0,))),
        preferred_element_type=jnp.float32,
    )


def attend_kernel(
    first, me_ref, sends_ref, own_ref, left_ref, order_ref, lower_ref, upper_ref, mixed_ref, all_ref
):
    rounds, _, tokens = order_ref.shape
    head = first + pl.program_id(0)
    spans = tokens // SPAN
    for r in range(rounds):
        spare = spare_span(sends_ref, r, head, me_ref[0])
        for at in range(2):
            tiles = [left_ref[r, 0, at, :, j] for j in range(SENT)]
            tiles.append(own_ref[r, 0, at, :, 0, spare])
            for j, tile in enumerate(tiles[:-1]):
                all_ref[r, at, :, j + (j > spare).astype(jnp.int32)] = tile
            all_ref[r, at, :, spare + 1] = tiles[-1]
        queries = as_spans(own_ref[r, 0, 0, :, 0])
        keys = jnp.concatenate([as_spans(all_ref[r, 0]), queries], axis=1)
        values = jnp.concatenate([as_spans(all_ref[r, 1]), as_spans(own_ref[r, 0, 1, :, 0])], axis=1)
        scores = batched(queries, keys, 2, 2)
        wide = keys.astype(jnp.float32)
        squares = wide * wide
        high = squares.astype(jnp.bfloat16)
        low = (squares - high.astype(jnp.float32)).astype(jnp.bfloat16)
        ones = jnp.ones((spans, 16, 2 * HEAD_DIM), jnp.bfloat16)
        sums = batched(ones, jnp.concatenate([high, low], axis=2), 2, 2)
        scaling = lax.rsqrt(sums[:, :1, :] + EPS) * (1.0 / math.sqrt(HEAD_DIM))
        scores = scores * scaling
        query_at = lax.broadcasted_iota(jnp.int32, scores.shape, 1)
        key_at = lax.broadcasted_iota(jnp.int32, scores.shape, 2)
        scores = jnp.where(key_at == query_at + SPAN, SELF_SCORE, scores)
        summit = jnp.max(scores, axis=-1, keepdims=True)
        raised = jnp.exp(scores - summit)
        totals = jnp.sum(raised, axis=-1, keepdims=True)
        weights = (raised * (1.0 / totals)).astype(jnp.bfloat16)
        mixed = batched(weights, values, 2, 1).astype(jnp.bfloat16)
        log_total = summit + jnp.log(totals)
        high = log_total.astype(jnp.bfloat16).astype(jnp.float32)
        middle = (log_total - high).astype(jnp.bfloat16).astype(jnp.float32)
        low = log_total - high - middle
        lane = lax.broadcasted_iota(jnp.int32, scores.shape, 2)
        terms = jnp.where(lane == 0, high, jnp.where(lane == 1, middle, low))
        terms = jnp.where(lane < 3, terms, 0.0).astype(jnp.bfloat16)
        mixed_ref[r, :, :HEAD_DIM] = mixed.reshape(tokens, HEAD_DIM)
        mixed_ref[r, :, HEAD_DIM:] = terms.reshape(tokens, HEAD_DIM)
    step = 256
    token_at = lax.broadcasted_iota(jnp.int32, (step, tokens), 0)
    for lower in range(0, tokens, step):
        rows, totals = [], []
        for r in range(rounds):
            onehot = order_ref[r, pl.ds(head, 1), :] == token_at + lower
            onehot = jnp.where(onehot, 1.0, 0.0).astype(jnp.bfloat16)
            found = jnp.dot(onehot, mixed_ref[r], preferred_element_type=jnp.float32)
            rows.append(found[:, :HEAD_DIM])
            totals.append(
                found[:, HEAD_DIM : HEAD_DIM + 1]
                + found[:, HEAD_DIM + 1 : HEAD_DIM + 2]
                + found[:, HEAD_DIM + 2 : HEAD_DIM + 3]
            )
        peak = functools.reduce(jnp.maximum, totals)
        shares = [jnp.exp(total - peak) for total in totals]
        inverse = 1.0 / functools.reduce(jnp.add, shares)
        blended = functools.reduce(
            jnp.add, [(share * inverse) * row for share, row in zip(shares, rows)]
        )
        out_ref = lower_ref if lower < tokens // 2 else upper_ref
        at = lower % (tokens // 2)
        out_ref[at : at + step, :] = blended.astype(jnp.bfloat16)


def attend(me, sends, own, left, order, pair):
    rounds, _, tokens = order.shape
    block = (rounds, 1, 2, QUARTERS, 1) + own.shape[5:]
    half = jax.ShapeDtypeStruct((tokens // 2, PAIR * HEAD_DIM), jnp.bfloat16)
    return pl.pallas_call(
        functools.partial(attend_kernel, PAIR * pair),
        grid=(PAIR,),
        in_specs=[
            pl.BlockSpec(memory_space=pltpu.SMEM),
            pl.BlockSpec(sends.shape, lambda h: (0, 0, 0, 0)),
            pl.BlockSpec(block, lambda h: (0, h, 0, 0, pair, 0, 0, 0)),
            pl.BlockSpec(block[:4] + left.shape[1:], lambda h: (0, h, 0, 0, 0, 0, 0)),
            pl.BlockSpec(order.shape, lambda h: (0, 0, 0)),
        ],
        out_specs=[pl.BlockSpec((tokens // 2, HEAD_DIM), lambda h: (0, h))] * 2,
        out_shape=[half, half],
        scratch_shapes=[
            pltpu.VMEM((rounds, tokens, 2 * HEAD_DIM), jnp.bfloat16),
            pltpu.VMEM((rounds, 2, QUARTERS) + own.shape[5:], jnp.bfloat16),
        ],
        compiler_params=params(),
        cost_estimate=pl.CostEstimate(
            flops=PAIR * rounds * tokens * 4 * HEAD_DIM * (tokens + 2 * SPAN),
            bytes_accessed=PAIR * rounds * tokens * 8 * HEAD_DIM,
            transcendentals=PAIR * rounds * tokens * 2 * SPAN,
        ),
    )(me, sends, own, left.reshape(own.shape[:4] + left.shape[1:]), order)


def output_kernel(started, *refs):
    out_ref = refs[-1]
    lower_half = pl.program_id(0) < pl.num_programs(0) // 2
    total = refs[0][...] if started else jnp.zeros(out_ref.shape, jnp.float32)
    for at in range(int(started), len(refs) - 1, 3):
        w_ref, lower_ref, upper_ref = refs[at : at + 3]
        rows = jnp.where(lower_half, lower_ref[...], upper_ref[...])
        total += jnp.dot(rows, w_ref[0], preferred_element_type=jnp.float32)
    out_ref[...] = total.astype(out_ref.dtype)


def project_out(weights, started, terms):
    columns = weights.shape[2]
    half, depth = terms[0][2].shape
    tokens = 2 * half
    steps = 4
    step = tokens // steps
    lower = lambda i: (jnp.minimum(i, steps // 2 - 1), 0)
    upper = lambda i: (jnp.maximum(i - steps // 2, 0), 0)
    in_specs, operands = [], []
    if started is not None:
        in_specs.append(pl.BlockSpec((step, columns), lambda i: (i, 0)))
        operands.append(started)
    for pair, behind, lower_rows, upper_rows in terms:
        in_specs += [
            pl.BlockSpec((1, depth, columns), lambda i, at=(behind, pair, 0): at),
            pl.BlockSpec((step, depth), lower),
            pl.BlockSpec((step, depth), upper),
        ]
        operands += [weights, lower_rows, upper_rows]
    kind = jnp.float32 if started is None else jnp.bfloat16
    return pl.pallas_call(
        functools.partial(output_kernel, started is not None),
        grid=(steps,),
        in_specs=in_specs,
        out_specs=pl.BlockSpec((step, columns), lambda i: (i, 0)),
        out_shape=jax.ShapeDtypeStruct((tokens, columns), kind),
        compiler_params=params(),
        cost_estimate=pl.CostEstimate(
            flops=2 * len(terms) * tokens * depth * columns,
            bytes_accessed=2 * len(terms) * depth * (tokens + columns) + 6 * tokens * columns,
            transcendentals=0,
        ),
    )(*operands)


def passed(array, by):
    count = lax.axis_size("head")
    return lax.ppermute(array, "head", [(i, (i + by) % count) for i in range(count)])


def from_all_groups(lower, upper, meanwhile=None):
    lower_behind = passed(lower, 1)
    upper_ahead = passed(upper, -1)
    upper_behind = passed(upper, 1)
    lower_ahead = passed(lower, -1)
    if meanwhile is not None:
        lower_behind, upper_ahead, meanwhile = lax.optimization_barrier(
            (lower_behind, upper_ahead, meanwhile)
        )
    lower_opposite = passed(lower_behind, 1)
    upper_opposite = passed(upper_ahead, -1)
    return meanwhile, [
        (0, lower, upper),
        (1, lower_behind, upper_behind),
        (3, lower_ahead, upper_ahead),
        (2, lower_opposite, upper_opposite),
    ]


def after(array, terms):
    array, rows = lax.optimization_barrier((array, [term[2:] for term in terms]))
    return array, [term[:2] + row for term, row in zip(terms, rows)]


def body(activations, w_qk, w_value, w_out, bucket_order, span_sends):
    seq_count = lax.axis_size("seq")
    head_count = lax.axis_size("head")
    my_seq = lax.axis_index("seq")
    my_head = lax.axis_index("head")
    me = my_seq.reshape(1).astype(jnp.int32)
    pairs = bucket_order.shape[1] // PAIR
    columns = w_out.shape[1] // head_count

    def send(pieces):
        return lax.all_to_all(pieces, "seq", split_axis=0, concat_axis=0, tiled=True)

    own, sent = project_and_sort(me, span_sends, activations, w_qk, w_value, bucket_order)
    arrived = send(sent.reshape(seq_count, pairs, SENT, QUARTER, HEAD_DIM))

    blocks = []
    for shift in range(head_count):
        at = lax.rem(my_head + shift, head_count) * columns
        block = lax.dynamic_slice_in_dim(w_out, at, columns, axis=1)
        blocks.append(passed(block, shift) if shift else block)
    weights = jnp.stack(blocks)

    of_round = span_sends[my_seq // (2 * PAIR * QUARTERS)]
    of_round = of_round.reshape((pairs, PAIR) + of_round.shape[1:])
    table = left_table(of_round[:, my_seq // (2 * QUARTERS) % PAIR])
    left = []
    for pair in range(pairs):
        pieces = permute(table, arrived, pair)
        pieces, arrived, weights = lax.optimization_barrier((pieces, arrived, weights))
        left.append(send(pieces))

    started, terms = None, []
    for pair in range(pairs):
        if terms:
            left[pair], terms = after(left[pair], terms)
        halves = attend(me, span_sends, own, left[pair], bucket_order, pair)
        if terms:
            started = project_out(weights, None, terms + [(pair, 0, *halves)])
        started, gathered = from_all_groups(*halves, started)
        terms = [(pair,) + term for term in gathered]
    return project_out(weights, started, terms[1:])


def solution(mesh):
    in_specs = (
        P("seq", None),
        P(None, "head"),
        P(None, "head"),
        P("head", None),
        P(None, "head", "seq"),
        P(None, "head", None, None),
    )
    out_specs = P("seq", "head")
    return jax.shard_map(body, mesh=mesh, in_specs=in_specs, out_specs=out_specs, check_vma=False)
```

time: 1000 us -> 188 us (0.19)
  local copies, waits for them, and re-layouts: 554 us -> 4.94 us
  waiting for transfers between devices: 231 us -> 80.9 us
  other arithmetic: 87.6 us -> 3.4 us
  matrix products: 65.7 us -> 0 us
  Pallas kernels: 0 us -> 56.7 us
  between operations: 14.5 us -> 0.24 us
    gather x38 -> x0, local copies, waits for them, and re-layouts: 449 us -> none  [the longest x24 434 us: take_rows(): blocks[positions]]
    all_to_all x6 -> x3, waiting for transfers between devices: 181 us -> 45.8 us  [send(): lax.all_to_all(pieces, 'seq', split_axis=0, concat_axis=0, tiled=True)]
    dot_general x7 -> x0, matrix products: 65.7 us -> none  [the longest x2 27.2 us: attend(): jnp.einsum('gpqe,gpke->gpqk', queries, key_part, preferred_element_type=j...]
    pallas_call x0 -> x7, Pallas kernels: none -> 56.7 us  [the longest x2 19.5 us: attend(): pl.pallas_call(functools.partial(attend_kernel, PAIR * pair), grid=(PAIR,...]
    reduce_scatter x1 -> x0, waiting for transfers between devices: 49.5 us -> none  [body(): lax.psum_scatter(partial_value.astype(jnp.bfloat16), 'head', scatter_dime...]
    ppermute x2 -> x15, waiting for transfers between devices: 0.01 us -> 35.2 us  [passed(): lax.ppermute(array, 'head', [(i, (i + by) % count) for i in range(count)])]
    concatenate x4 -> x1, other arithmetic: 30.7 us -> 0.08 us  [left_table(): wrapped = jnp.roll(last, 1, axis=-1)]
    unnamed x37 -> x24, local copies, waits for them, and re-layouts: 32.4 us -> 2.82 us
  transfers between devices with their start and end apart: 9 -> 18, of which waited for: 5 -> 11; matrix products, arithmetic and copies ran while one was open for 29% -> 3% of each run, Pallas kernels for 0% -> 11%
where the time goes in v1:
time: 188 us; the launch traced here: 187 us
  waiting for transfers between devices  80.9 us (43%)
  Pallas kernels  56.7 us (30%)
  starting transfers between devices  41 us (22%)
  local copies, waits for them, and re-layouts  4.94 us (3%)
  other arithmetic  3.4 us (2%)
    all_to_all x3, waiting for transfers between devices, send(): lax.all_to_all(pieces, 'seq', split_axis=0, concat_axis=0, tiled=True)  45.8 us
    ppermute x15, waiting for transfers between devices, passed(): lax.ppermute(array, 'head', [(i, (i + by) % count) for i in range(count)])  35.2 us
    ppermute x15, starting transfers between devices, passed(): lax.ppermute(array, 'head', [(i, (i + by) % count) for i in range(count)])  23.8 us
    pallas_call x2, Pallas kernels, attend(): pl.pallas_call(functools.partial(attend_kernel, PAIR * pair), grid=(PAIR,...  19.5 us
    all_to_all x3, starting transfers between devices, send(): lax.all_to_all(pieces, 'seq', split_axis=0, concat_axis=0, tiled=True)  17.2 us
    pallas_call x1, Pallas kernels, project_and_sort(): pl.pallas_call(sort_kernel, grid=(heads,), in_specs=[pl.BlockSpec(memory_...  17.1 us
    pallas_call x2, Pallas kernels, project_out(): pl.pallas_call(functools.partial(output_kernel, started is not None), gri...  10.6 us
    pallas_call x2, Pallas kernels, permute(): pl.pallas_call(functools.partial(permute_kernel, pair), grid=(steps,), in...  9.41 us
  transfers between devices with their start and end apart: 18, of which 11 were waited for; matrix products, arithmetic and copies ran while one was open for 3% of the time, Pallas kernels for 11%

profile of v1, /device:TPU:0, one launch (start us, length us, event | category | flops | bytes accessed | tf_op | source)
XLA Modules:
  0.0 187.2 jit_solution(10590426607485138757)
XLA Ops:
  0.0 17.1 %shard_map.64 = (bf16[2,2,2,4,2,16,16,128]{7,6,5,4,3,2,1,0:T(8,128)(2,1)}, bf16[2,2,2,4,2,15,16,128]{7,6,5,4,3,2,1,0:T(8,128)(2,1)}) custom-call(s32[1]{0:T(128)} %bitcast.me_ref, s32[2,4,32,32]{3,2,1,0:T(8,128)} %sends_ref.5, bf16[1024,2048]{1,0:T(8,128)(2,1)} %act_ref.1, bf16[2048,512]{1,0:T(8,128)(2,1)} %wq_ref.1, bf16[2048,512]{1,0:T(8,128)(2,1)} %wv_ref.1, ...), custom_call_target="tpu_custom_call" | custom-call | flops 8589934592 | bytes 12582912 | tf_op jit(solution)/shard_map/pallas_call | solution.py:80
  17.1 7.7 %all-to-all-start = ((bf16[32,2,15,16,128]{4,3,2,1,0:T(8,128)(2,1)}), bf16[32,2,15,16,128]{4,3,2,1,0:T(8,128)(2,1)}, u32[]{:S(2)}, u32[]{:S(2)}) async-start(bf16[32,2,15,16,128]{4,3,2,1,0:T(8,128)(2,1)} %bitcast.17), calls=%async_computation | async-start | bytes 7864320 | tf_op jit(solution)/shard_map/all_to_all | solution.py:376
  28.0 2.1 %collective-permute-start.2 = (bf16[512,512]{1,0:T(8,128)(2,1)}, bf16[512,512]{1,0:T(8,128)(2,1)S(1)}, u32[]{:S(2)}, u32[]{:S(2)}) collective-permute-start(bf16[512,512]{1,0:T(8,128)(2,1)} %get-tuple-element.57), channel_id=1, source_target_pairs={{0,3},{1,0},{2,1},{3,2},{4,7},{5,4},{6,5},{7,6},{8,11},{9,8},{10,9... | collective-permute-start | bytes 1572872 | tf_op jit(solution)/shard_map/ppermute | solution.py:339
  34.7 7.9 %collective-permute-done = bf16[512,512]{1,0:T(8,128)(2,1)S(1)} collective-permute-done((bf16[512,512]{1,0:T(8,128)(2,1)}, bf16[512,512]{1,0:T(8,128)(2,1)S(1)}, u32[]{:S(2)}, u32[]{:S(2)}) %collective-permute-start) | collective-permute-done | bytes 524320 | tf_op jit(solution)/shard_map/ppermute | solution.py:339
  42.6 10.6 %collective-permute-done.2 = bf16[512,512]{1,0:T(8,128)(2,1)S(1)} collective-permute-done((bf16[512,512]{1,0:T(8,128)(2,1)}, bf16[512,512]{1,0:T(8,128)(2,1)S(1)}, u32[]{:S(2)}, u32[]{:S(2)}) %collective-permute-start.2) | collective-permute-done | bytes 524320 | tf_op jit(solution)/shard_map/ppermute | solution.py:339
  56.6 18.8 %all-to-all-done.in_ref = bf16[32,2,15,16,128]{4,3,2,1,0:T(8,128)(2,1)} async-done(((bf16[32,2,15,16,128]{4,3,2,1,0:T(8,128)(2,1)}), bf16[32,2,15,16,128]{4,3,2,1,0:T(8,128)(2,1)}, u32[]{:S(2)}, u32[]{:S(2)}) %all-to-all-start) | async-done | bytes 3932192 | tf_op jit(solution)/shard_map/all_to_all | solution.py:376
  75.4 4.6 %shard_map.65 = bf16[32,15,16,128]{3,2,1,0:T(8,128)(2,1)} custom-call(s32[2,480]{1,0:T(2,128)} %min.12.table_ref, bf16[32,2,15,16,128]{4,3,2,1,0:T(8,128)(2,1)} %all-to-all-done.in_ref), custom_call_target="tpu_custom_call" | custom-call | flops 983040 | bytes 3932160 | tf_op jit(solution)/shard_map/pallas_call | solution.py:166
  80.0 4.7 %all-to-all-start.2 = ((bf16[32,15,16,128]{3,2,1,0:T(8,128)(2,1)}), bf16[32,15,16,128]{3,2,1,0:T(8,128)(2,1)}, u32[]{:S(2)}, u32[]{:S(2)}) async-start(bf16[32,15,16,128]{3,2,1,0:T(8,128)(2,1)} %shard_map.65), calls=%async_computation.2 | async-start | bytes 3932160 | tf_op jit(solution)/shard_map/all_to_all | solution.py:376
  84.8 4.8 %shard_map.66 = bf16[32,15,16,128]{3,2,1,0:T(8,128)(2,1)} custom-call(s32[2,480]{1,0:T(2,128)} %min.12.table_ref, bf16[32,2,15,16,128]{4,3,2,1,0:T(8,128)(2,1)} %all-to-all-done.in_ref), custom_call_target="tpu_custom_call" | custom-call | flops 983040 | bytes 3932160 | tf_op jit(solution)/shard_map/pallas_call | solution.py:166
  89.5 23.6 %all-to-all-done.2 = bf16[32,15,16,128]{3,2,1,0:T(8,128)(2,1)} async-done(((bf16[32,15,16,128]{3,2,1,0:T(8,128)(2,1)}), bf16[32,15,16,128]{3,2,1,0:T(8,128)(2,1)}, u32[]{:S(2)}, u32[]{:S(2)}) %all-to-all-start.2) | async-done | bytes 1966112 | tf_op jit(solution)/shard_map/all_to_all | solution.py:376
  113.2 4.7 %all-to-all-start.1 = ((bf16[32,15,16,128]{3,2,1,0:T(8,128)(2,1)}), bf16[32,15,16,128]{3,2,1,0:T(8,128)(2,1)}, u32[]{:S(2)}, u32[]{:S(2)}) async-start(bf16[32,15,16,128]{3,2,1,0:T(8,128)(2,1)} %shard_map.66), calls=%async_computation.1 | async-start | bytes 3932160 | tf_op jit(solution)/shard_map/all_to_all | solution.py:376
  117.9 9.8 %shard_map.67 = (bf16[512,256]{1,0:T(8,128)(2,1)}, bf16[512,256]{1,0:T(8,128)(2,1)}) custom-call(s32[1]{0:T(128)} %bitcast.me_ref, s32[2,4,32,32]{3,2,1,0:T(8,128)} %sends_ref.5, bf16[2,2,2,4,2,16,16,128]{7,6,5,4,3,2,1,0:T(8,128)(2,1)} %get-tuple-element.28.own_ref, bf16[2,2,2,4,15,16,128]{6,5,4,3,2,1,0:T(8,128)(2,1)} %bitcast.8.left_ref, ...), custom_call_target="tpu_custom_call" | custom-call | flops 2415919104 | bytes 4194304 | tf_op jit(solution)/shard_map/pallas_call | solution.py:266
  129.6 2.2 %collective-permute-start.6 = (bf16[512,256]{1,0:T(8,128)(2,1)}, bf16[512,256]{1,0:T(8,128)(2,1)S(1)}, u32[]{:S(2)}, u32[]{:S(2)}) collective-permute-start(bf16[512,256]{1,0:T(8,128)(2,1)} %get-tuple-element.41.refs_2_), channel_id=1, source_target_pairs={{0,3},{1,0},{2,1},{3,2},{4,7},{5,4},{6,5},{7,6},{8,11},{9,8},{10,9... | collective-permute-start | bytes 786440 | tf_op jit(solution)/shard_map/ppermute | solution.py:339
  131.8 2.0 %collective-permute-start.5 = (bf16[512,256]{1,0:T(8,128)(2,1)}, bf16[512,256]{1,0:T(8,128)(2,1)S(1)}, u32[]{:S(2)}, u32[]{:S(2)}) collective-permute-start(bf16[512,256]{1,0:T(8,128)(2,1)} %get-tuple-element.40.refs_1_), channel_id=1, source_target_pairs={{0,3},{1,0},{2,1},{3,2},{4,7},{5,4},{6,5},{7,6},{8,11},{9,8},{10,9... | collective-permute-start | bytes 786440 | tf_op jit(solution)/shard_map/ppermute | solution.py:339
  133.8 5.2 %collective-permute-done.3.refs_4_ = bf16[512,256]{1,0:T(8,128)(2,1)S(1)} collective-permute-done((bf16[512,256]{1,0:T(8,128)(2,1)}, bf16[512,256]{1,0:T(8,128)(2,1)S(1)}, u32[]{:S(2)}, u32[]{:S(2)}) %collective-permute-start.3) | collective-permute-done | bytes 262176 | tf_op jit(solution)/shard_map/ppermute | solution.py:339
  139.8 3.2 %collective-permute-start.8 = (bf16[512,256]{1,0:T(8,128)(2,1)S(1)}, bf16[512,256]{1,0:T(8,128)(2,1)S(1)}, u32[]{:S(2)}, u32[]{:S(2)}) collective-permute-start(bf16[512,256]{1,0:T(8,128)(2,1)S(1)} %collective-permute-done.6.refs_8_), channel_id=1, source_target_pairs={{0,3},{1,0},{2,1},{3,2},{4,7},{5,4},{6,5},{7,6},{8,11},{9,8},{10,9... | collective-permute-start | bytes 786440 | tf_op jit(solution)/shard_map/ppermute | solution.py:339
  143.0 3.3 %all-to-all-done.1 = bf16[32,15,16,128]{3,2,1,0:T(8,128)(2,1)} async-done(((bf16[32,15,16,128]{3,2,1,0:T(8,128)(2,1)}), bf16[32,15,16,128]{3,2,1,0:T(8,128)(2,1)}, u32[]{:S(2)}, u32[]{:S(2)}) %all-to-all-start.1) | async-done | bytes 1966112 | tf_op jit(solution)/shard_map/all_to_all | solution.py:376
  146.4 3.4 %collective-permute-done.7.refs_10_ = bf16[512,256]{1,0:T(8,128)(2,1)S(1)} collective-permute-done((bf16[512,256]{1,0:T(8,128)(2,1)S(1)}, bf16[512,256]{1,0:T(8,128)(2,1)S(1)}, u32[]{:S(2)}, u32[]{:S(2)}) %collective-permute-start.7) | collective-permute-done | bytes 262176 | tf_op jit(solution)/shard_map/ppermute | solution.py:339
  151.2 9.8 %shard_map.68 = (bf16[512,256]{1,0:T(8,128)(2,1)}, bf16[512,256]{1,0:T(8,128)(2,1)}) custom-call(s32[1]{0:T(128)} %bitcast.me_ref, s32[2,4,32,32]{3,2,1,0:T(8,128)} %sends_ref.5, bf16[2,2,2,4,2,16,16,128]{7,6,5,4,3,2,1,0:T(8,128)(2,1)} %get-tuple-element.28.own_ref, bf16[2,2,2,4,15,16,128]{6,5,4,3,2,1,0:T(8,128)(2,1)} %bitcast.9.left_ref, ...), custom_call_target="tpu_custom_call" | custom-call | flops 2415919104 | bytes 4194304 | tf_op jit(solution)/shard_map/pallas_call | solution.py:266
  161.5 2.7 %collective-permute-start.10 = (bf16[512,256]{1,0:T(8,128)(2,1)}, bf16[512,256]{1,0:T(8,128)(2,1)S(1)}, u32[]{:S(2)}, u32[]{:S(2)}) collective-permute-start(bf16[512,256]{1,0:T(8,128)(2,1)} %get-tuple-element.38.refs_14_), channel_id=1, source_target_pairs={{0,3},{1,0},{2,1},{3,2},{4,7},{5,4},{6,5},{7,6},{8,11},{9,8},{10,9... | collective-permute-start | bytes 786440 | tf_op jit(solution)/shard_map/ppermute | solution.py:339
  166.2 5.6 %shard_map.69.refs_0_ = f32[1024,512]{1,0:T(8,128)} custom-call(bf16[4,512,512]{2,1,0:T(8,128)(2,1)} %pad_maximum_fusion.refs_0_.refs_3_.refs_6_.refs_9_.refs_12_.refs_1_.refs_4_.refs_7_, bf16[512,256]{1,0:T(8,128)(2,1)} %get-tuple-element.40.refs_1_, bf16[512,256]{1,0:T(8,128)(2,1)} %get-tuple-element.41.refs_2_, ...), custom_call_target="tpu_custom_call" | custom-call | flops 1342177280 | bytes 7077888 | tf_op jit(solution)/shard_map/pallas_call | solution.py:322
  172.6 2.6 %collective-permute-start.14 = (bf16[512,256]{1,0:T(8,128)(2,1)S(1)}, bf16[512,256]{1,0:T(8,128)(2,1)}, u32[]{:S(2)}, u32[]{:S(2)}) collective-permute-start(bf16[512,256]{1,0:T(8,128)(2,1)S(1)} %collective-permute-done.10.refs_6_), channel_id=1, source_target_pairs={{0,3},{1,0},{2,1},{3,2},{4,7},{5,4},{6,5},{7,6},{8,11},{9,8},{10,9... | collective-permute-start | bytes 786440 | tf_op jit(solution)/shard_map/ppermute | solution.py:339
  177.3 4.1 %collective-permute-done.13.refs_8_ = bf16[512,256]{1,0:T(8,128)(2,1)S(1)} collective-permute-done((bf16[512,256]{1,0:T(8,128)(2,1)S(1)}, bf16[512,256]{1,0:T(8,128)(2,1)S(1)}, u32[]{:S(2)}, u32[]{:S(2)}) %collective-permute-start.13) | collective-permute-done | bytes 262176 | tf_op jit(solution)/shard_map/ppermute | solution.py:339
  182.1 5.1 %shard_map.70 = bf16[1024,512]{1,0:T(8,128)(2,1)} custom-call(f32[1024,512]{1,0:T(8,128)} %shard_map.69.refs_0_, bf16[4,512,512]{2,1,0:T(8,128)(2,1)} %pad_maximum_fusion.refs_0_.refs_3_.refs_6_.refs_9_.refs_12_.refs_1_.refs_4_.refs_7_, bf16[512,256]{1,0:T(8,128)(2,1)} %copy-done.1, bf16[512,256]{1,0:T(8,128)(2,1)} %collective-permute-done.11.refs_3_, ...), custom_call_target="tpu_custom_call" | custom-call | flops 805306368 | bytes 5505024 | tf_op jit(solution)/shard_map/pallas_call | solution.py:322
  (62 shorter events, 21.4 us)
Async XLA Ops:
  17.1 7.7 %copy-start = (bf16[512,2048]{1,0:T(8,128)(2,1)S(1)}, bf16[512,2048]{1,0:T(8,128)(2,1)}, u32[]{:S(2)}) copy-start(bf16[512,2048]{1,0:T(8,128)(2,1)} %param.9) | copy-start | bytes 6291460
  17.1 58.3 %all-to-all-start = ((bf16[32,2,15,16,128]{4,3,2,1,0:T(8,128)(2,1)}), bf16[32,2,15,16,128]{4,3,2,1,0:T(8,128)(2,1)}, u32[]{:S(2)}, u32[]{:S(2)}) async-start(bf16[32,2,15,16,128]{4,3,2,1,0:T(8,128)(2,1)} %bitcast.17), calls=%async_computation | async-start | bytes 7864320 | tf_op jit(solution)/shard_map/all_to_all | solution.py:376
  24.8 7.2 %copy-start.11 = (s32[2,4,32,32]{3,2,1,0:T(8,128)S(1)}, s32[2,4,32,32]{3,2,1,0:T(8,128)}, u32[]{:S(2)}) copy-start(s32[2,4,32,32]{3,2,1,0:T(8,128)} %sends_ref.5) | copy-start | bytes 98308
  26.1 16.5 %collective-permute-start = (bf16[512,512]{1,0:T(8,128)(2,1)}, bf16[512,512]{1,0:T(8,128)(2,1)S(1)}, u32[]{:S(2)}, u32[]{:S(2)}) collective-permute-start(bf16[512,512]{1,0:T(8,128)(2,1)} %get-tuple-element.56), channel_id=1, source_target_pairs={{0,1},{1,2},{2,3},{3,0},{4,5},{5,6},{6,7},{7,4},{8,9},{9,10},{10,1... | collective-permute-start | bytes 1572872 | tf_op jit(solution)/shard_map/ppermute | solution.py:339
  28.0 25.3 %collective-permute-start.2 = (bf16[512,512]{1,0:T(8,128)(2,1)}, bf16[512,512]{1,0:T(8,128)(2,1)S(1)}, u32[]{:S(2)}, u32[]{:S(2)}) collective-permute-start(bf16[512,512]{1,0:T(8,128)(2,1)} %get-tuple-element.57), channel_id=1, source_target_pairs={{0,3},{1,0},{2,1},{3,2},{4,7},{5,4},{6,5},{7,6},{8,11},{9,8},{10,9... | collective-permute-start | bytes 1572872 | tf_op jit(solution)/shard_map/ppermute | solution.py:339
  30.1 24.9 %collective-permute-start.1 = (bf16[512,512]{1,0:T(8,128)(2,1)S(1)}, bf16[512,512]{1,0:T(8,128)(2,1)S(1)}, u32[]{:S(2)}, u32[]{:S(2)}) collective-permute-start(bf16[512,512]{1,0:T(8,128)(2,1)S(1)} %get-tuple-element.58), channel_id=1, source_target_pairs={{0,2},{1,3},{2,0},{3,1},{4,6},{5,7},{6,4},{7,5},{8,10},{9,11},{10,... | collective-permute-start | bytes 1572872 | tf_op jit(solution)/shard_map/ppermute | solution.py:339
  80.0 33.2 %all-to-all-start.2 = ((bf16[32,15,16,128]{3,2,1,0:T(8,128)(2,1)}), bf16[32,15,16,128]{3,2,1,0:T(8,128)(2,1)}, u32[]{:S(2)}, u32[]{:S(2)}) async-start(bf16[32,15,16,128]{3,2,1,0:T(8,128)(2,1)} %shard_map.65), calls=%async_computation.2 | async-start | bytes 3932160 | tf_op jit(solution)/shard_map/all_to_all | solution.py:376
  113.2 33.2 %all-to-all-start.1 = ((bf16[32,15,16,128]{3,2,1,0:T(8,128)(2,1)}), bf16[32,15,16,128]{3,2,1,0:T(8,128)(2,1)}, u32[]{:S(2)}, u32[]{:S(2)}) async-start(bf16[32,15,16,128]{3,2,1,0:T(8,128)(2,1)} %shard_map.66), calls=%async_computation.1 | async-start | bytes 3932160 | tf_op jit(solution)/shard_map/all_to_all | solution.py:376
  127.7 11.3 %collective-permute-start.3 = (bf16[512,256]{1,0:T(8,128)(2,1)}, bf16[512,256]{1,0:T(8,128)(2,1)S(1)}, u32[]{:S(2)}, u32[]{:S(2)}) collective-permute-start(bf16[512,256]{1,0:T(8,128)(2,1)} %get-tuple-element.40.refs_1_), channel_id=1, source_target_pairs={{0,1},{1,2},{2,3},{3,0},{4,5},{5,6},{6,7},{7,4},{8,9},{9,10},{10,1... | collective-permute-start | bytes 786440 | tf_op jit(solution)/shard_map/ppermute | solution.py:339
  129.6 10.1 %collective-permute-start.6 = (bf16[512,256]{1,0:T(8,128)(2,1)}, bf16[512,256]{1,0:T(8,128)(2,1)S(1)}, u32[]{:S(2)}, u32[]{:S(2)}) collective-permute-start(bf16[512,256]{1,0:T(8,128)(2,1)} %get-tuple-element.41.refs_2_), channel_id=1, source_target_pairs={{0,3},{1,0},{2,1},{3,2},{4,7},{5,4},{6,5},{7,6},{8,11},{9,8},{10,9... | collective-permute-start | bytes 786440 | tf_op jit(solution)/shard_map/ppermute | solution.py:339
  131.8 14.5 %collective-permute-start.5 = (bf16[512,256]{1,0:T(8,128)(2,1)}, bf16[512,256]{1,0:T(8,128)(2,1)S(1)}, u32[]{:S(2)}, u32[]{:S(2)}) collective-permute-start(bf16[512,256]{1,0:T(8,128)(2,1)} %get-tuple-element.40.refs_1_), channel_id=1, source_target_pairs={{0,3},{1,0},{2,1},{3,2},{4,7},{5,4},{6,5},{7,6},{8,11},{9,8},{10,9... | collective-permute-start | bytes 786440 | tf_op jit(solution)/shard_map/ppermute | solution.py:339
  133.8 12.6 %collective-permute-start.4 = (bf16[512,256]{1,0:T(8,128)(2,1)}, bf16[512,256]{1,0:T(8,128)(2,1)S(1)}, u32[]{:S(2)}, u32[]{:S(2)}) collective-permute-start(bf16[512,256]{1,0:T(8,128)(2,1)} %get-tuple-element.41.refs_2_), channel_id=1, source_target_pairs={{0,1},{1,2},{2,3},{3,0},{4,5},{5,6},{6,7},{7,4},{8,9},{9,10},{10,1... | collective-permute-start | bytes 786440 | tf_op jit(solution)/shard_map/ppermute | solution.py:339
  139.8 10.0 %collective-permute-start.7 = (bf16[512,256]{1,0:T(8,128)(2,1)S(1)}, bf16[512,256]{1,0:T(8,128)(2,1)S(1)}, u32[]{:S(2)}, u32[]{:S(2)}) collective-permute-start(bf16[512,256]{1,0:T(8,128)(2,1)S(1)} %collective-permute-done.3.refs_4_), channel_id=1, source_target_pairs={{0,1},{1,2},{2,3},{3,0},{4,5},{5,6},{6,7},{7,4},{8,9},{9,10},{10,1... | collective-permute-start | bytes 786440 | tf_op jit(solution)/shard_map/ppermute | solution.py:339
  139.8 10.0 %copy-start.6 = (bf16[512,256]{1,0:T(8,128)(2,1)}, bf16[512,256]{1,0:T(8,128)(2,1)S(1)}, u32[]{:S(2)}) copy-start(bf16[512,256]{1,0:T(8,128)(2,1)S(1)} %collective-permute-done.6.refs_8_) | copy-start | bytes 786436
  139.8 10.0 %collective-permute-start.8 = (bf16[512,256]{1,0:T(8,128)(2,1)S(1)}, bf16[512,256]{1,0:T(8,128)(2,1)S(1)}, u32[]{:S(2)}, u32[]{:S(2)}) collective-permute-start(bf16[512,256]{1,0:T(8,128)(2,1)S(1)} %collective-permute-done.6.refs_8_), channel_id=1, source_target_pairs={{0,3},{1,0},{2,1},{3,2},{4,7},{5,4},{6,5},{7,6},{8,11},{9,8},{10,9... | collective-permute-start | bytes 786440 | tf_op jit(solution)/shard_map/ppermute | solution.py:339
  160.9 10.8 %collective-permute-start.9 = (bf16[512,256]{1,0:T(8,128)(2,1)}, bf16[512,256]{1,0:T(8,128)(2,1)S(1)}, u32[]{:S(2)}, u32[]{:S(2)}) collective-permute-start(bf16[512,256]{1,0:T(8,128)(2,1)} %get-tuple-element.37.refs_13_), channel_id=1, source_target_pairs={{0,1},{1,2},{2,3},{3,0},{4,5},{5,6},{6,7},{7,4},{8,9},{9,10},{10,1... | collective-permute-start | bytes 786440 | tf_op jit(solution)/shard_map/ppermute | solution.py:339
  161.5 10.3 %collective-permute-start.10 = (bf16[512,256]{1,0:T(8,128)(2,1)}, bf16[512,256]{1,0:T(8,128)(2,1)S(1)}, u32[]{:S(2)}, u32[]{:S(2)}) collective-permute-start(bf16[512,256]{1,0:T(8,128)(2,1)} %get-tuple-element.38.refs_14_), channel_id=1, source_target_pairs={{0,3},{1,0},{2,1},{3,2},{4,7},{5,4},{6,5},{7,6},{8,11},{9,8},{10,9... | collective-permute-start | bytes 786440 | tf_op jit(solution)/shard_map/ppermute | solution.py:339
  164.2 12.5 %collective-permute-start.12 = (bf16[512,256]{1,0:T(8,128)(2,1)}, bf16[512,256]{1,0:T(8,128)(2,1)S(1)}, u32[]{:S(2)}, u32[]{:S(2)}) collective-permute-start(bf16[512,256]{1,0:T(8,128)(2,1)} %get-tuple-element.37.refs_13_), channel_id=1, source_target_pairs={{0,3},{1,0},{2,1},{3,2},{4,7},{5,4},{6,5},{7,6},{8,11},{9,8},{10,9... | collective-permute-start | bytes 786440 | tf_op jit(solution)/shard_map/ppermute | solution.py:339
  165.3 12.0 %collective-permute-start.11 = (bf16[512,256]{1,0:T(8,128)(2,1)}, bf16[512,256]{1,0:T(8,128)(2,1)}, u32[]{:S(2)}, u32[]{:S(2)}) collective-permute-start(bf16[512,256]{1,0:T(8,128)(2,1)} %get-tuple-element.38.refs_14_), channel_id=1, source_target_pairs={{0,1},{1,2},{2,3},{3,0},{4,5},{5,6},{6,7},{7,4},{8,9},{9,10},{10,1... | collective-permute-start | bytes 786440 | tf_op jit(solution)/shard_map/ppermute | solution.py:339
  171.8 10.3 %copy-start.1 = (bf16[512,256]{1,0:T(8,128)(2,1)}, bf16[512,256]{1,0:T(8,128)(2,1)S(1)}, u32[]{:S(2)}) copy-start(bf16[512,256]{1,0:T(8,128)(2,1)S(1)} %collective-permute-done.9.refs_2_) | copy-start | bytes 786436
  171.8 10.3 %copy-start.2 = (bf16[512,256]{1,0:T(8,128)(2,1)}, bf16[512,256]{1,0:T(8,128)(2,1)S(1)}, u32[]{:S(2)}) copy-start(bf16[512,256]{1,0:T(8,128)(2,1)S(1)} %collective-permute-done.10.refs_6_) | copy-start | bytes 786436
  171.8 9.6 %collective-permute-start.13 = (bf16[512,256]{1,0:T(8,128)(2,1)S(1)}, bf16[512,256]{1,0:T(8,128)(2,1)S(1)}, u32[]{:S(2)}, u32[]{:S(2)}) collective-permute-start(bf16[512,256]{1,0:T(8,128)(2,1)S(1)} %collective-permute-done.9.refs_2_), channel_id=1, source_target_pairs={{0,1},{1,2},{2,3},{3,0},{4,5},{5,6},{6,7},{7,4},{8,9},{9,10},{10,1... | collective-permute-start | bytes 786440 | tf_op jit(solution)/shard_map/ppermute | solution.py:339
  172.6 9.5 %collective-permute-start.14 = (bf16[512,256]{1,0:T(8,128)(2,1)S(1)}, bf16[512,256]{1,0:T(8,128)(2,1)}, u32[]{:S(2)}, u32[]{:S(2)}) collective-permute-start(bf16[512,256]{1,0:T(8,128)(2,1)S(1)} %collective-permute-done.10.refs_6_), channel_id=1, source_target_pairs={{0,3},{1,0},{2,1},{3,2},{4,7},{5,4},{6,5},{7,6},{8,11},{9,8},{10,9... | collective-permute-start | bytes 786440 | tf_op jit(solution)/shard_map/ppermute | solution.py:339
  176.7 5.4 %copy-start.3 = (bf16[512,256]{1,0:T(8,128)(2,1)}, bf16[512,256]{1,0:T(8,128)(2,1)S(1)}, u32[]{:S(2)}) copy-start(bf16[512,256]{1,0:T(8,128)(2,1)S(1)} %collective-permute-done.12.refs_5_) | copy-start | bytes 786436
  (6 other events, 9.7 us)

commit v2 on v1

--- a/solution.py
+++ b/solution.py
@@ -16,11 +16,12 @@
 QUARTERS = SPAN // QUARTER
 PAIR = 2
 SENT = 15
-VMEM_LIMIT = 63 * 1024 * 1024
-
-
-def params(**kwargs):
-    return pltpu.CompilerParams(vmem_limit_bytes=VMEM_LIMIT, **kwargs)
+VMEM_LIMIT = 64 * 1024 * 1024
+OUTPUT_LIMIT = 24 * 1024 * 1024
+
+
+def params(limit=VMEM_LIMIT):
+    return pltpu.CompilerParams(vmem_limit_bytes=limit)
 
 
 def spare_span(sends_ref, r, head, me):
@@ -32,12 +33,12 @@
 
 
 def sort_kernel(
-    me_ref, sends_ref, act_ref, wq_ref, wv_ref, order_ref, out_ref, sent_ref, kv_ref, onehot_ref
+    first, me_ref, sends_ref, act_ref, wq_ref, wv_ref, order_ref, out_ref, sent_ref, kv_ref, onehot_ref
 ):
     tokens = act_ref.shape[0]
     spans = tokens // SPAN
     rounds = out_ref.shape[0]
-    head = pl.program_id(0)
+    head = first + pl.program_id(0)
     lanes = 128
     token_at = lax.broadcasted_iota(jnp.int32, (lanes, tokens), 1).astype(jnp.float32)
     for r in range(rounds):
@@ -72,20 +73,21 @@
     lax.fori_loop(0, rounds, one_round, 0)
 
 
-def project_and_sort(me, sends, activations, w_qk, w_value, order):
+def project_and_sort(me, sends, activations, w_qk, w_value, order, pair):
     tokens, width = activations.shape
-    rounds, heads = order.shape[:2]
+    rounds, heads = order.shape[0], PAIR
+    first = PAIR * pair
     block = (rounds, 1, 2, QUARTERS, 1, tokens // SPAN, QUARTER, HEAD_DIM)
     shape = (rounds, PAIR, 2, QUARTERS, heads // PAIR) + block[5:]
     return pl.pallas_call(
-        sort_kernel,
+        functools.partial(sort_kernel, first),
         grid=(heads,),
         in_specs=[
             pl.BlockSpec(memory_space=pltpu.SMEM),
             pl.BlockSpec(sends.shape, lambda h: (0, 0, 0, 0)),
             pl.BlockSpec((tokens, width), lambda h: (0, 0)),
-            pl.BlockSpec((width, HEAD_DIM), lambda h: (0, h)),
-            pl.BlockSpec((width, HEAD_DIM), lambda h: (0, h)),
+            pl.BlockSpec((width, HEAD_DIM), lambda h: (0, first + h)),
+            pl.BlockSpec((width, HEAD_DIM), lambda h: (0, first + h)),
             pl.BlockSpec(order.shape, lambda h: (0, 0, 0)),
         ],
         out_specs=[
@@ -156,19 +158,19 @@
             out_ref[t, k] = tile
         return carry
 
-    lax.fori_loop(0, steps, one_block, 0)
+    lax.fori_loop(0, steps, one_block, 0, unroll=4)
 
 
 def permute(table, pieces, pair):
     blocks, _, sent, rows, columns = pieces.shape
-    steps = 4
+    steps = 2
     size = blocks * sent * rows * columns
     return pl.pallas_call(
         functools.partial(permute_kernel, pair),
         grid=(steps,),
         in_specs=[
             pl.BlockSpec(memory_space=pltpu.SMEM),
-            pl.BlockSpec((blocks, 1, sent, rows, columns), lambda i: (0, pair, 0, 0, 0)),
+            pl.BlockSpec((blocks, 1, sent, rows, columns), lambda i: (0, 0, 0, 0, 0)),
         ],
         out_specs=pl.BlockSpec((blocks // steps, sent, rows, columns), lambda i: (i, 0, 0, 0)),
         out_shape=jax.ShapeDtypeStruct((blocks, sent, rows, columns), jnp.bfloat16),
@@ -192,8 +194,9 @@
 
 
 def attend_kernel(
-    first, me_ref, sends_ref, own_ref, left_ref, order_ref, lower_ref, upper_ref, mixed_ref, all_ref
+    first, me_ref, sends_ref, own_ref, left_ref, order_ref, *refs
 ):
+    *out_refs, mixed_ref, all_ref = refs
     rounds, _, tokens = order_ref.shape
     head = first + pl.program_id(0)
     spans = tokens // SPAN
@@ -211,11 +214,8 @@
         scores = batched(queries, keys, 2, 2)
         wide = keys.astype(jnp.float32)
         squares = wide * wide
-        high = squares.astype(jnp.bfloat16)
-        low = (squares - high.astype(jnp.float32)).astype(jnp.bfloat16)
-        ones = jnp.ones((spans, 16, 2 * HEAD_DIM), jnp.bfloat16)
-        sums = batched(ones, jnp.concatenate([high, low], axis=2), 2, 2)
-        scaling = lax.rsqrt(sums[:, :1, :] + EPS) * (1.0 / math.sqrt(HEAD_DIM))
+        sums = jnp.sum(squares, axis=2)[:, None, :]
+        scaling = lax.rsqrt(sums + EPS) * (1.0 / math.sqrt(HEAD_DIM))
         scores = scores * scaling
         query_at = lax.broadcasted_iota(jnp.int32, scores.shape, 1)
         key_at = lax.broadcasted_iota(jnp.int32, scores.shape, 2)
@@ -254,27 +254,28 @@
         blended = functools.reduce(
             jnp.add, [(share * inverse) * row for share, row in zip(shares, rows)]
         )
-        out_ref = lower_ref if lower < tokens // 2 else upper_ref
-        at = lower % (tokens // 2)
+        share = tokens // len(out_refs)
+        out_ref, at = out_refs[lower // share], lower % share
         out_ref[at : at + step, :] = blended.astype(jnp.bfloat16)
 
 
-def attend(me, sends, own, left, order, pair):
+def attend(me, sends, own, left, order, pair, parts):
     rounds, _, tokens = order.shape
     block = (rounds, 1, 2, QUARTERS, 1) + own.shape[5:]
-    half = jax.ShapeDtypeStruct((tokens // 2, PAIR * HEAD_DIM), jnp.bfloat16)
+    share = tokens // parts
+    part = jax.ShapeDtypeStruct((share, PAIR * HEAD_DIM), jnp.bfloat16)
     return pl.pallas_call(
         functools.partial(attend_kernel, PAIR * pair),
         grid=(PAIR,),
         in_specs=[
             pl.BlockSpec(memory_space=pltpu.SMEM),
             pl.BlockSpec(sends.shape, lambda h: (0, 0, 0, 0)),
-            pl.BlockSpec(block, lambda h: (0, h, 0, 0, pair, 0, 0, 0)),
+            pl.BlockSpec(block, lambda h: (0, h, 0, 0, 0, 0, 0, 0)),
             pl.BlockSpec(block[:4] + left.shape[1:], lambda h: (0, h, 0, 0, 0, 0, 0)),
             pl.BlockSpec(order.shape, lambda h: (0, 0, 0)),
         ],
-        out_specs=[pl.BlockSpec((tokens // 2, HEAD_DIM), lambda h: (0, h))] * 2,
-        out_shape=[half, half],
+        out_specs=[pl.BlockSpec((share, HEAD_DIM), lambda h: (0, h))] * parts,
+        out_shape=[part] * parts,
         scratch_shapes=[
             pltpu.VMEM((rounds, tokens, 2 * HEAD_DIM), jnp.bfloat16),
             pltpu.VMEM((rounds, 2, QUARTERS) + own.shape[5:], jnp.bfloat16),
@@ -288,44 +289,46 @@
     )(me, sends, own, left.reshape(own.shape[:4] + left.shape[1:]), order)
 
 
-def output_kernel(started, *refs):
+def output_kernel(started, parts, *refs):
     out_ref = refs[-1]
     lower_half = pl.program_id(0) < pl.num_programs(0) // 2
     total = refs[0][...] if started else jnp.zeros(out_ref.shape, jnp.float32)
-    for at in range(int(started), len(refs) - 1, 3):
-        w_ref, lower_ref, upper_ref = refs[at : at + 3]
-        rows = jnp.where(lower_half, lower_ref[...], upper_ref[...])
-        total += jnp.dot(rows, w_ref[0], preferred_element_type=jnp.float32)
+    at = int(started)
+    for count in parts:
+        rows = refs[at + 1][...]
+        if count == 2:
+            rows = jnp.where(lower_half, rows, refs[at + 2][...])
+        total += jnp.dot(rows, refs[at][0], preferred_element_type=jnp.float32)
+        at += 1 + count
     out_ref[...] = total.astype(out_ref.dtype)
 
 
 def project_out(weights, started, terms):
     columns = weights.shape[2]
-    half, depth = terms[0][2].shape
-    tokens = 2 * half
-    steps = 4
+    tokens = sum(rows.shape[0] for rows in terms[0][2])
+    depth = terms[0][2][0].shape[1]
+    steps = 2
     step = tokens // steps
+    whole = lambda i: (i, 0)
     lower = lambda i: (jnp.minimum(i, steps // 2 - 1), 0)
     upper = lambda i: (jnp.maximum(i - steps // 2, 0), 0)
     in_specs, operands = [], []
     if started is not None:
-        in_specs.append(pl.BlockSpec((step, columns), lambda i: (i, 0)))
+        in_specs.append(pl.BlockSpec((step, columns), whole))
         operands.append(started)
-    for pair, behind, lower_rows, upper_rows in terms:
-        in_specs += [
-            pl.BlockSpec((1, depth, columns), lambda i, at=(behind, pair, 0): at),
-            pl.BlockSpec((step, depth), lower),
-            pl.BlockSpec((step, depth), upper),
-        ]
-        operands += [weights, lower_rows, upper_rows]
+    for pair, behind, rows in terms:
+        in_specs.append(pl.BlockSpec((1, depth, columns), lambda i, at=(behind, pair, 0): at))
+        for where in [whole] if len(rows) == 1 else [lower, upper]:
+            in_specs.append(pl.BlockSpec((step, depth), where))
+        operands += [weights, *rows]
     kind = jnp.float32 if started is None else jnp.bfloat16
     return pl.pallas_call(
-        functools.partial(output_kernel, started is not None),
+        functools.partial(output_kernel, started is not None, [len(t[2]) for t in terms]),
         grid=(steps,),
         in_specs=in_specs,
-        out_specs=pl.BlockSpec((step, columns), lambda i: (i, 0)),
+        out_specs=pl.BlockSpec((step, columns), whole),
         out_shape=jax.ShapeDtypeStruct((tokens, columns), kind),
-        compiler_params=params(),
+        compiler_params=params(OUTPUT_LIMIT),
         cost_estimate=pl.CostEstimate(
             flops=2 * len(terms) * tokens * depth * columns,
             bytes_accessed=2 * len(terms) * depth * (tokens + columns) + 6 * tokens * columns,
@@ -339,28 +342,25 @@
     return lax.ppermute(array, "head", [(i, (i + by) % count) for i in range(count)])
 
 
-def from_all_groups(lower, upper, meanwhile=None):
+def from_all_groups(mine):
+    return [(0, [mine]), (1, [passed(mine, 1)]), (3, [passed(mine, -1)]), (2, [passed(mine, 2)])]
+
+
+def round_the_ring(lower, upper, meanwhile):
     lower_behind = passed(lower, 1)
     upper_ahead = passed(upper, -1)
     upper_behind = passed(upper, 1)
     lower_ahead = passed(lower, -1)
-    if meanwhile is not None:
-        lower_behind, upper_ahead, meanwhile = lax.optimization_barrier(
-            (lower_behind, upper_ahead, meanwhile)
-        )
+    lower_behind, upper_ahead, meanwhile = lax.optimization_barrier(
+        (lower_behind, upper_ahead, meanwhile)
+    )
     lower_opposite = passed(lower_behind, 1)
     upper_opposite = passed(upper_ahead, -1)
     return meanwhile, [
-        (0, lower, upper),
-        (1, lower_behind, upper_behind),
-        (3, lower_ahead, upper_ahead),
-        (2, lower_opposite, upper_opposite),
+        (1, [lower_behind, upper_behind]),
+        (3, [lower_ahead, upper_ahead]),
+        (2, [lower_opposite, upper_opposite]),
     ]
-
-
-def after(array, terms):
-    array, rows = lax.optimization_barrier((array, [term[2:] for term in terms]))
-    return array, [term[:2] + row for term, row in zip(terms, rows)]
 
 
 def body(activations, w_qk, w_value, w_out, bucket_order, span_sends):
@@ -375,8 +375,13 @@
     def send(pieces):
         return lax.all_to_all(pieces, "seq", split_axis=0, concat_axis=0, tiled=True)
 
-    own, sent = project_and_sort(me, span_sends, activations, w_qk, w_value, bucket_order)
-    arrived = send(sent.reshape(seq_count, pairs, SENT, QUARTER, HEAD_DIM))
+    own, arrived = [], []
+    for pair in range(pairs):
+        rows, sent = project_and_sort(
+            me, span_sends, activations, w_qk, w_value, bucket_order, pair
+        )
+        own.append(rows)
+        arrived.append(send(sent.reshape(seq_count, 1, SENT, QUARTER, HEAD_DIM)))
 
     blocks = []
     for shift in range(head_count):
@@ -390,20 +395,22 @@
     table = left_table(of_round[:, my_seq // (2 * QUARTERS) % PAIR])
     left = []
     for pair in range(pairs):
-        pieces = permute(table, arrived, pair)
-        pieces, arrived, weights = lax.optimization_barrier((pieces, arrived, weights))
+        pieces = permute(table, arrived[pair], pair)
+        pieces, arrived[-1], weights = lax.optimization_barrier((pieces, arrived[-1], weights))
         left.append(send(pieces))
 
-    started, terms = None, []
-    for pair in range(pairs):
-        if terms:
-            left[pair], terms = after(left[pair], terms)
-        halves = attend(me, span_sends, own, left[pair], bucket_order, pair)
-        if terms:
-            started = project_out(weights, None, terms + [(pair, 0, *halves)])
-        started, gathered = from_all_groups(*halves, started)
-        terms = [(pair,) + term for term in gathered]
-    return project_out(weights, started, terms[1:])
+    def attended(pair, parts):
+        return attend(me, span_sends, own[pair], left[pair], bucket_order, pair, parts)
+
+    (mine,) = attended(0, 1)
+    terms = from_all_groups(mine)
+    left[1], rows = lax.optimization_barrier((left[1], [rows for _, rows in terms[:1]]))
+    terms[:1] = [(term[0], row) for term, row in zip(terms, rows)]
+    halves = attended(1, 2)
+    terms = [(0, *term) for term in terms] + [(1, 0, halves)]
+    started = project_out(weights, None, terms)
+    started, terms = round_the_ring(*halves, started)
+    return project_out(weights, started, [(1, *term) for term in terms])
 
 
 def solution(mesh):

time: 188 us -> 179 us (0.952)
  waiting for transfers between devices: 80.9 us -> 69.6 us
  Pallas kernels: 56.7 us -> 52.3 us
  local copies, waits for them, and re-layouts: 4.94 us -> 7.41 us
  starting transfers between devices: 41 us -> 43.4 us
  other arithmetic: 3.4 us -> 5.35 us
    ppermute x15 -> x12, waiting for transfers between devices: 35.2 us -> 4.35 us  [passed(): lax.ppermute(array, 'head', [(i, (i + by) % count) for i in range(count)])]
    all_to_all x3 -> x4, waiting for transfers between devices: 45.8 us -> 65.3 us  [send(): lax.all_to_all(pieces, 'seq', split_axis=0, concat_axis=0, tiled=True)]
    all_to_all x3 -> x4, starting transfers between devices: 17.2 us -> 22.2 us  [send(): lax.all_to_all(pieces, 'seq', split_axis=0, concat_axis=0, tiled=True)]
    ppermute x15 -> x12, starting transfers between devices: 23.8 us -> 21.2 us  [passed(): lax.ppermute(array, 'head', [(i, (i + by) % count) for i in range(count)])]
    unnamed x24 -> x22, local copies, waits for them, and re-layouts: 2.82 us -> 5.16 us
    pallas_call x3 -> x4, Pallas kernels: 27.7 us -> 25.7 us  [the longest x2 20.8 us: project_and_sort(): pl.pallas_call(functools.partial(sort_kernel, first), grid=(heads,), in_s...]
  transfers between devices with their start and end apart: 18 -> 16, of which waited for: 11 -> 5; matrix products, arithmetic and copies ran while one was open for 3% -> 4% of each run, Pallas kernels for 11% -> 22%
where the time goes in v2:
time: 179 us; the launch traced here: 178 us
  waiting for transfers between devices  69.6 us (39%)
  Pallas kernels  52.3 us (29%)
  starting transfers between devices  43.4 us (24%)
  local copies, waits for them, and re-layouts  7.41 us (4%)
  other arithmetic  5.35 us (3%)
    all_to_all x4, waiting for transfers between devices, send(): lax.all_to_all(pieces, 'seq', split_axis=0, concat_axis=0, tiled=True)  65.3 us
    all_to_all x4, starting transfers between devices, send(): lax.all_to_all(pieces, 'seq', split_axis=0, concat_axis=0, tiled=True)  22.2 us
    ppermute x12, starting transfers between devices, passed(): lax.ppermute(array, 'head', [(i, (i + by) % count) for i in range(count)])  21.2 us
    pallas_call x2, Pallas kernels, project_and_sort(): pl.pallas_call(functools.partial(sort_kernel, first), grid=(heads,), in_s...  20.8 us
    pallas_call x2, Pallas kernels, attend(): pl.pallas_call(functools.partial(attend_kernel, PAIR * pair), grid=(PAIR,...  17.9 us
    pallas_call x2, Pallas kernels, permute(): pl.pallas_call(functools.partial(permute_kernel, pair), grid=(steps,), in...  8.68 us
    unnamed x22, local copies, waits for them, and re-layouts  5.16 us
    pallas_call x2, Pallas kernels, project_out(): pl.pallas_call(functools.partial(output_kernel, started is not None, [len...  4.93 us
  transfers between devices with their start and end apart: 16, of which 5 were waited for; matrix products, arithmetic and copies ran while one was open for 4% of the time, Pallas kernels for 22%

profile of v2, /device:TPU:0, one launch (start us, length us, event | category | flops | bytes accessed | tf_op | source)
XLA Modules:
  0.0 178.3 jit_solution(12030777841498174817)
XLA Ops:
  0.0 10.4 %shard_map.65 = (bf16[2,2,2,4,1,16,16,128]{7,6,5,4,3,2,1,0:T(8,128)(2,1)}, bf16[2,2,2,4,1,15,16,128]{7,6,5,4,3,2,1,0:T(8,128)(2,1)}) custom-call(s32[1]{0:T(128)} %bitcast.me_ref, s32[2,4,32,32]{3,2,1,0:T(8,128)} %sends_ref.7, bf16[1024,2048]{1,0:T(8,128)(2,1)} %act_ref.3, bf16[2048,512]{1,0:T(8,128)(2,1)} %wq_ref.3, bf16[2048,512]{1,0:T(8,128)(2,1)} %wv_ref.3, ...), custom_call_target="tpu_custom_call" | custom-call | flops 4294967296 | bytes 8388608 | tf_op jit(solution)/shard_map/pallas_call | solution.py:82
  10.4 7.7 %all-to-all-start = ((bf16[32,1,15,16,128]{4,3,2,1,0:T(8,128)(2,1)}), bf16[32,1,15,16,128]{4,3,2,1,0:T(8,128)(2,1)}, u32[]{:S(2)}, u32[]{:S(2)}) async-start(bf16[32,1,15,16,128]{4,3,2,1,0:T(8,128)(2,1)} %bitcast.18), calls=%async_computation | async-start | bytes 3932160 | tf_op jit(solution)/shard_map/all_to_all | solution.py:376
  21.4 2.1 %collective-permute-start.2 = (bf16[512,512]{1,0:T(8,128)(2,1)}, bf16[512,512]{1,0:T(8,128)(2,1)}, u32[]{:S(2)}, u32[]{:S(2)}) collective-permute-start(bf16[512,512]{1,0:T(8,128)(2,1)} %get-tuple-element.43), channel_id=1, source_target_pairs={{0,3},{1,0},{2,1},{3,2},{4,7},{5,4},{6,5},{7,6},{8,11},{9,8},{10,9... | collective-permute-start | bytes 1572872 | tf_op jit(solution)/shard_map/ppermute | solution.py:342
  27.0 10.4 %shard_map.64 = (bf16[2,2,2,4,1,16,16,128]{7,6,5,4,3,2,1,0:T(8,128)(2,1)}, bf16[2,2,2,4,1,15,16,128]{7,6,5,4,3,2,1,0:T(8,128)(2,1)}) custom-call(s32[1]{0:T(128)} %bitcast.me_ref, s32[2,4,32,32]{3,2,1,0:T(8,128)} %sends_ref.7, bf16[1024,2048]{1,0:T(8,128)(2,1)} %act_ref.3, bf16[2048,512]{1,0:T(8,128)(2,1)} %wq_ref.3, bf16[2048,512]{1,0:T(8,128)(2,1)} %wv_ref.3, ...), custom_call_target="tpu_custom_call" | custom-call | flops 4294967296 | bytes 8388608 | tf_op jit(solution)/shard_map/pallas_call | solution.py:82
  37.4 9.1 %all-to-all-done.in_ref = bf16[32,1,15,16,128]{4,3,2,1,0:T(8,128)(2,1)} async-done(((bf16[32,1,15,16,128]{4,3,2,1,0:T(8,128)(2,1)}), bf16[32,1,15,16,128]{4,3,2,1,0:T(8,128)(2,1)}, u32[]{:S(2)}, u32[]{:S(2)}) %all-to-all-start) | async-done | bytes 1966112 | tf_op jit(solution)/shard_map/all_to_all | solution.py:376
  46.5 4.9 %all-to-all-start.1 = ((bf16[32,1,15,16,128]{4,3,2,1,0:T(8,128)(2,1)}), bf16[32,1,15,16,128]{4,3,2,1,0:T(8,128)(2,1)}, u32[]{:S(2)}, u32[]{:S(2)}) async-start(bf16[32,1,15,16,128]{4,3,2,1,0:T(8,128)(2,1)} %bitcast.19), calls=%async_computation.1 | async-start | bytes 3932160 | tf_op jit(solution)/shard_map/all_to_all | solution.py:376
  53.7 3.0 %pad_maximum_fusion.refs_0_.refs_2_.refs_4_.refs_6_.refs_8_.refs_1_.refs_7_ = bf16[4,512,512]{2,1,0:T(8,128)(2,1)} fusion(bf16[1,512,512]{2,1,0:T(8,128)(2,1)} %bitcast.8, bf16[1,512,512]{2,1,0:T(8,128)(2,1)} %bitcast.7, bf16[1,512,512]{2,1,0:T(8,128)(2,1)} %bitcast.6, bf16[1,512,512]{2,1,0:T(8,128)(2,1)S(1)} %copy-done.6), kind=kLoop, calls=%fused_computation | loop fusion | flops 3145728 | bytes 4194304 | tf_op jit(solution)/shard_map/stack | solution.py:391
  56.7 4.3 %shard_map.66 = bf16[32,15,16,128]{3,2,1,0:T(8,128)(2,1)} custom-call(s32[2,480]{1,0:T(2,128)} %min.12.table_ref, bf16[32,1,15,16,128]{4,3,2,1,0:T(8,128)(2,1)} %all-to-all-done.in_ref), custom_call_target="tpu_custom_call" | custom-call | flops 983040 | bytes 3932160 | tf_op jit(solution)/shard_map/pallas_call | solution.py:168
  61.0 18.8 %all-to-all-done.1.in_ref = bf16[32,1,15,16,128]{4,3,2,1,0:T(8,128)(2,1)} async-done(((bf16[32,1,15,16,128]{4,3,2,1,0:T(8,128)(2,1)}), bf16[32,1,15,16,128]{4,3,2,1,0:T(8,128)(2,1)}, u32[]{:S(2)}, u32[]{:S(2)}) %all-to-all-start.1) | async-done | bytes 1966112 | tf_op jit(solution)/shard_map/all_to_all | solution.py:376
  79.8 4.7 %all-to-all-start.3 = ((bf16[32,15,16,128]{3,2,1,0:T(8,128)(2,1)}), bf16[32,15,16,128]{3,2,1,0:T(8,128)(2,1)}, u32[]{:S(2)}, u32[]{:S(2)}) async-start(bf16[32,15,16,128]{3,2,1,0:T(8,128)(2,1)} %shard_map.66), calls=%async_computation.3 | async-start | bytes 3932160 | tf_op jit(solution)/shard_map/all_to_all | solution.py:376
  84.5 4.4 %shard_map.67 = bf16[32,15,16,128]{3,2,1,0:T(8,128)(2,1)} custom-call(s32[2,480]{1,0:T(2,128)} %min.12.table_ref, bf16[32,1,15,16,128]{4,3,2,1,0:T(8,128)(2,1)} %all-to-all-done.1.in_ref), custom_call_target="tpu_custom_call" | custom-call | flops 983040 | bytes 3932160 | tf_op jit(solution)/shard_map/pallas_call | solution.py:168
  88.9 24.0 %all-to-all-done.3 = bf16[32,15,16,128]{3,2,1,0:T(8,128)(2,1)} async-done(((bf16[32,15,16,128]{3,2,1,0:T(8,128)(2,1)}), bf16[32,15,16,128]{3,2,1,0:T(8,128)(2,1)}, u32[]{:S(2)}, u32[]{:S(2)}) %all-to-all-start.3) | async-done | bytes 1966112 | tf_op jit(solution)/shard_map/all_to_all | solution.py:376
  113.0 4.9 %all-to-all-start.2 = ((bf16[32,15,16,128]{3,2,1,0:T(8,128)(2,1)}), bf16[32,15,16,128]{3,2,1,0:T(8,128)(2,1)}, u32[]{:S(2)}, u32[]{:S(2)}) async-start(bf16[32,15,16,128]{3,2,1,0:T(8,128)(2,1)} %shard_map.67), calls=%async_computation.2 | async-start | bytes 3932160 | tf_op jit(solution)/shard_map/all_to_all | solution.py:376
  117.9 9.0 %shard_map.68.refs_1_ = bf16[1024,256]{1,0:T(8,128)(2,1)} custom-call(s32[1]{0:T(128)} %bitcast.me_ref, s32[2,4,32,32]{3,2,1,0:T(8,128)} %sends_ref.7, bf16[2,2,2,4,1,16,16,128]{7,6,5,4,3,2,1,0:T(8,128)(2,1)} %get-tuple-element.27.own_ref, bf16[2,2,2,4,15,16,128]{6,5,4,3,2,1,0:T(8,128)(2,1)} %bitcast.9.left_ref, s32[2,4,1024]{2,1,0:T(4,128)} %order_ref.7), custom_call_target="tpu_custom_call" | custom-call | flops 2415919104 | bytes 4194304 | tf_op jit(solution)/shard_map/pallas_call | solution.py:267
  126.9 3.9 %collective-permute-start.7 = (bf16[1024,256]{1,0:T(8,128)(2,1)}, bf16[1024,256]{1,0:T(8,128)(2,1)}, u32[]{:S(2)}, u32[]{:S(2)}) collective-permute-start(bf16[1024,256]{1,0:T(8,128)(2,1)} %shard_map.68.refs_1_), channel_id=1, source_target_pairs={{0,2},{1,3},{2,0},{3,1},{4,6},{5,7},{6,4},{7,5},{8,10},{9,11},{10,... | collective-permute-start | bytes 1572872 | tf_op jit(solution)/shard_map/ppermute | solution.py:342
  132.8 13.4 %all-to-all-done.2 = bf16[32,15,16,128]{3,2,1,0:T(8,128)(2,1)} async-done(((bf16[32,15,16,128]{3,2,1,0:T(8,128)(2,1)}), bf16[32,15,16,128]{3,2,1,0:T(8,128)(2,1)}, u32[]{:S(2)}, u32[]{:S(2)}) %all-to-all-start.2) | async-done | bytes 1966112 | tf_op jit(solution)/shard_map/all_to_all | solution.py:376
  146.1 8.9 %shard_map.69 = (bf16[512,256]{1,0:T(8,128)(2,1)}, bf16[512,256]{1,0:T(8,128)(2,1)}) custom-call(s32[1]{0:T(128)} %bitcast.me_ref, s32[2,4,32,32]{3,2,1,0:T(8,128)} %sends_ref.7, bf16[2,2,2,4,1,16,16,128]{7,6,5,4,3,2,1,0:T(8,128)(2,1)} %get-tuple-element.21.own_ref, bf16[2,2,2,4,15,16,128]{6,5,4,3,2,1,0:T(8,128)(2,1)} %bitcast.10.left_ref, ...), custom_call_target="tpu_custom_call" | custom-call | flops 2415919104 | bytes 4194304 | tf_op jit(solution)/shard_map/pallas_call | solution.py:267
  155.0 1.9 %collective-permute-start.3 = (bf16[512,256]{1,0:T(8,128)(2,1)}, bf16[512,256]{1,0:T(8,128)(2,1)S(1)}, u32[]{:S(2)}, u32[]{:S(2)}) collective-permute-start(bf16[512,256]{1,0:T(8,128)(2,1)} %get-tuple-element.30.refs_9_), channel_id=1, source_target_pairs={{0,1},{1,2},{2,3},{3,0},{4,5},{5,6},{6,7},{7,4},{8,9},{9,10},{10,1... | collective-permute-start | bytes 786440 | tf_op jit(solution)/shard_map/ppermute | solution.py:342
  156.9 2.2 %collective-permute-start.4 = (bf16[512,256]{1,0:T(8,128)(2,1)}, bf16[512,256]{1,0:T(8,128)(2,1)S(1)}, u32[]{:S(2)}, u32[]{:S(2)}) collective-permute-start(bf16[512,256]{1,0:T(8,128)(2,1)} %get-tuple-element.31.refs_10_), channel_id=1, source_target_pairs={{0,3},{1,0},{2,1},{3,2},{4,7},{5,4},{6,5},{7,6},{8,11},{9,8},{10,9... | collective-permute-start | bytes 786440 | tf_op jit(solution)/shard_map/ppermute | solution.py:342
  159.1 2.0 %collective-permute-start.9 = (bf16[512,256]{1,0:T(8,128)(2,1)}, bf16[512,256]{1,0:T(8,128)(2,1)S(1)}, u32[]{:S(2)}, u32[]{:S(2)}) collective-permute-start(bf16[512,256]{1,0:T(8,128)(2,1)} %get-tuple-element.30.refs_9_), channel_id=1, source_target_pairs={{0,3},{1,0},{2,1},{3,2},{4,7},{5,4},{6,5},{7,6},{8,11},{9,8},{10,9... | collective-permute-start | bytes 786440 | tf_op jit(solution)/shard_map/ppermute | solution.py:342
  165.7 3.0 %shard_map.70.refs_0_ = f32[1024,512]{1,0:T(8,128)S(1)} custom-call(bf16[4,512,512]{2,1,0:T(8,128)(2,1)S(1)} %copy-done, bf16[1024,256]{1,0:T(8,128)(2,1)S(1)} %copy-done.2, bf16[4,512,512]{2,1,0:T(8,128)(2,1)S(1)} %copy-done, bf16[1024,256]{1,0:T(8,128)(2,1)} %collective-permute-done.5.refs_3_, bf16[4,512,512]{2,1,0:T(8,128)(2,1)S(1)} %copy-done, ...), custom_call_target="tpu_custom_call" | custom-call | flops 1342177280 | bytes 7077888 | tf_op jit(solution)/shard_map/pallas_call | solution.py:325
  168.8 3.2 %collective-permute-start.11 = (bf16[512,256]{1,0:T(8,128)(2,1)S(1)}, bf16[512,256]{1,0:T(8,128)(2,1)S(1)}, u32[]{:S(2)}, u32[]{:S(2)}) collective-permute-start(bf16[512,256]{1,0:T(8,128)(2,1)S(1)} %collective-permute-done.4.refs_6_), channel_id=1, source_target_pairs={{0,3},{1,0},{2,1},{3,2},{4,7},{5,4},{6,5},{7,6},{8,11},{9,8},{10,9... | collective-permute-start | bytes 786440 | tf_op jit(solution)/shard_map/ppermute | solution.py:342
  172.0 4.3 %collective-permute-done.10.refs_8_ = bf16[512,256]{1,0:T(8,128)(2,1)S(1)} collective-permute-done((bf16[512,256]{1,0:T(8,128)(2,1)S(1)}, bf16[512,256]{1,0:T(8,128)(2,1)S(1)}, u32[]{:S(2)}, u32[]{:S(2)}) %collective-permute-start.10) | collective-permute-done | bytes 262176 | tf_op jit(solution)/shard_map/ppermute | solution.py:342
  176.4 2.0 %shard_map.71 = bf16[1024,512]{1,0:T(8,128)(2,1)} custom-call(f32[1024,512]{1,0:T(8,128)S(1)} %shard_map.70.refs_0_, bf16[4,512,512]{2,1,0:T(8,128)(2,1)S(1)} %copy-done.1, bf16[512,256]{1,0:T(8,128)(2,1)S(1)} %collective-permute-done.3.refs_2_, bf16[512,256]{1,0:T(8,128)(2,1)S(1)} %collective-permute-done.8.refs_3_, bf16[4,512,512]{2,1,0:T(8,128)(2,1)S(1)} %copy-done.1, ...), custom_call_target="tpu_custom_call" | custom-call | flops 805306368 | bytes 5505024 | tf_op jit(solution)/shard_map/pallas_call | solution.py:325
  (57 shorter events, 15.8 us)
Async XLA Ops:
  10.4 7.7 %copy-start.5 = (bf16[512,2048]{1,0:T(8,128)(2,1)S(1)}, bf16[512,2048]{1,0:T(8,128)(2,1)}, u32[]{:S(2)}) copy-start(bf16[512,2048]{1,0:T(8,128)(2,1)} %param.9) | copy-start | bytes 6291460
  10.4 36.1 %all-to-all-start = ((bf16[32,1,15,16,128]{4,3,2,1,0:T(8,128)(2,1)}), bf16[32,1,15,16,128]{4,3,2,1,0:T(8,128)(2,1)}, u32[]{:S(2)}, u32[]{:S(2)}) async-start(bf16[32,1,15,16,128]{4,3,2,1,0:T(8,128)(2,1)} %bitcast.18), calls=%async_computation | async-start | bytes 3932160 | tf_op jit(solution)/shard_map/all_to_all | solution.py:376
  18.1 7.3 %copy-start.10 = (s32[2,4,32,32]{3,2,1,0:T(8,128)S(1)}, s32[2,4,32,32]{3,2,1,0:T(8,128)}, u32[]{:S(2)}) copy-start(s32[2,4,32,32]{3,2,1,0:T(8,128)} %sends_ref.7) | copy-start | bytes 98308
  19.5 34.2 %collective-permute-start = (bf16[512,512]{1,0:T(8,128)(2,1)}, bf16[512,512]{1,0:T(8,128)(2,1)}, u32[]{:S(2)}, u32[]{:S(2)}) collective-permute-start(bf16[512,512]{1,0:T(8,128)(2,1)} %get-tuple-element.42), channel_id=1, source_target_pairs={{0,1},{1,2},{2,3},{3,0},{4,5},{5,6},{6,7},{7,4},{8,9},{9,10},{10,1... | collective-permute-start | bytes 1572872 | tf_op jit(solution)/shard_map/ppermute | solution.py:342
  21.4 32.3 %collective-permute-start.2 = (bf16[512,512]{1,0:T(8,128)(2,1)}, bf16[512,512]{1,0:T(8,128)(2,1)}, u32[]{:S(2)}, u32[]{:S(2)}) collective-permute-start(bf16[512,512]{1,0:T(8,128)(2,1)} %get-tuple-element.43), channel_id=1, source_target_pairs={{0,3},{1,0},{2,1},{3,2},{4,7},{5,4},{6,5},{7,6},{8,11},{9,8},{10,9... | collective-permute-start | bytes 1572872 | tf_op jit(solution)/shard_map/ppermute | solution.py:342
  23.5 30.2 %collective-permute-start.1 = (bf16[512,512]{1,0:T(8,128)(2,1)}, bf16[512,512]{1,0:T(8,128)(2,1)}, u32[]{:S(2)}, u32[]{:S(2)}) collective-permute-start(bf16[512,512]{1,0:T(8,128)(2,1)} %get-tuple-element.44), channel_id=1, source_target_pairs={{0,2},{1,3},{2,0},{3,1},{4,6},{5,7},{6,4},{7,5},{8,10},{9,11},{10,... | collective-permute-start | bytes 1572872 | tf_op jit(solution)/shard_map/ppermute | solution.py:342
  37.4 14.0 %copy-start.7 = (s32[2,32,32]{2,1,0:T(8,128)S(1)}, s32[2,32,32]{2,1,0:T(8,128)}, u32[]{:S(2)}) copy-start(s32[2,32,32]{2,1,0:T(8,128)} %select_reduce_fusion.1) | copy-start | bytes 24580
  37.4 14.0 %copy-start.9 = (s32[1,4,32,32]{3,2,1,0:T(8,128)S(1)}, s32[1,4,32,32]{3,2,1,0:T(8,128)}, u32[]{:S(2)}) copy-start(s32[1,4,32,32]{3,2,1,0:T(8,128)} %copy-done.8) | copy-start | bytes 49156
  46.5 7.2 %copy-start.6 = (bf16[1,512,512]{2,1,0:T(8,128)(2,1)S(1)}, bf16[1,512,512]{2,1,0:T(8,128)(2,1)}, u32[]{:S(2)}) copy-start(bf16[1,512,512]{2,1,0:T(8,128)(2,1)} %get-tuple-element.41) | copy-start | bytes 1572868
  46.5 33.3 %all-to-all-start.1 = ((bf16[32,1,15,16,128]{4,3,2,1,0:T(8,128)(2,1)}), bf16[32,1,15,16,128]{4,3,2,1,0:T(8,128)(2,1)}, u32[]{:S(2)}, u32[]{:S(2)}) async-start(bf16[32,1,15,16,128]{4,3,2,1,0:T(8,128)(2,1)} %bitcast.19), calls=%async_computation.1 | async-start | bytes 3932160 | tf_op jit(solution)/shard_map/all_to_all | solution.py:376
  79.8 33.2 %all-to-all-start.3 = ((bf16[32,15,16,128]{3,2,1,0:T(8,128)(2,1)}), bf16[32,15,16,128]{3,2,1,0:T(8,128)(2,1)}, u32[]{:S(2)}, u32[]{:S(2)}) async-start(bf16[32,15,16,128]{3,2,1,0:T(8,128)(2,1)} %shard_map.66), calls=%async_computation.3 | async-start | bytes 3932160 | tf_op jit(solution)/shard_map/all_to_all | solution.py:376
  113.0 33.2 %all-to-all-start.2 = ((bf16[32,15,16,128]{3,2,1,0:T(8,128)(2,1)}), bf16[32,15,16,128]{3,2,1,0:T(8,128)(2,1)}, u32[]{:S(2)}, u32[]{:S(2)}) async-start(bf16[32,15,16,128]{3,2,1,0:T(8,128)(2,1)} %shard_map.67), calls=%async_computation.2 | async-start | bytes 3932160 | tf_op jit(solution)/shard_map/all_to_all | solution.py:376
  126.9 32.3 %collective-permute-start.7 = (bf16[1024,256]{1,0:T(8,128)(2,1)}, bf16[1024,256]{1,0:T(8,128)(2,1)}, u32[]{:S(2)}, u32[]{:S(2)}) collective-permute-start(bf16[1024,256]{1,0:T(8,128)(2,1)} %shard_map.68.refs_1_), channel_id=1, source_target_pairs={{0,2},{1,3},{2,0},{3,1},{4,6},{5,7},{6,4},{7,5},{8,10},{9,11},{10,... | collective-permute-start | bytes 1572872 | tf_op jit(solution)/shard_map/ppermute | solution.py:342
  130.7 30.4 %collective-permute-start.6 = (bf16[1024,256]{1,0:T(8,128)(2,1)}, bf16[1024,256]{1,0:T(8,128)(2,1)}, u32[]{:S(2)}, u32[]{:S(2)}) collective-permute-start(bf16[1024,256]{1,0:T(8,128)(2,1)} %shard_map.68.refs_1_), channel_id=1, source_target_pairs={{0,3},{1,0},{2,1},{3,2},{4,7},{5,4},{6,5},{7,6},{8,11},{9,8},{10,9... | collective-permute-start | bytes 1572872 | tf_op jit(solution)/shard_map/ppermute | solution.py:342
  131.4 29.7 %collective-permute-start.5 = (bf16[1024,256]{1,0:T(8,128)(2,1)}, bf16[1024,256]{1,0:T(8,128)(2,1)}, u32[]{:S(2)}, u32[]{:S(2)}) collective-permute-start(bf16[1024,256]{1,0:T(8,128)(2,1)} %shard_map.68.refs_1_), channel_id=1, source_target_pairs={{0,1},{1,2},{2,3},{3,0},{4,5},{5,6},{6,7},{7,4},{8,9},{9,10},{10,1... | collective-permute-start | bytes 1572872 | tf_op jit(solution)/shard_map/ppermute | solution.py:342
  155.0 13.7 %collective-permute-start.3 = (bf16[512,256]{1,0:T(8,128)(2,1)}, bf16[512,256]{1,0:T(8,128)(2,1)S(1)}, u32[]{:S(2)}, u32[]{:S(2)}) collective-permute-start(bf16[512,256]{1,0:T(8,128)(2,1)} %get-tuple-element.30.refs_9_), channel_id=1, source_target_pairs={{0,1},{1,2},{2,3},{3,0},{4,5},{5,6},{6,7},{7,4},{8,9},{9,10},{10,1... | collective-permute-start | bytes 786440 | tf_op jit(solution)/shard_map/ppermute | solution.py:342
  156.9 11.8 %collective-permute-start.4 = (bf16[512,256]{1,0:T(8,128)(2,1)}, bf16[512,256]{1,0:T(8,128)(2,1)S(1)}, u32[]{:S(2)}, u32[]{:S(2)}) collective-permute-start(bf16[512,256]{1,0:T(8,128)(2,1)} %get-tuple-element.31.refs_10_), channel_id=1, source_target_pairs={{0,3},{1,0},{2,1},{3,2},{4,7},{5,4},{6,5},{7,6},{8,11},{9,8},{10,9... | collective-permute-start | bytes 786440 | tf_op jit(solution)/shard_map/ppermute | solution.py:342
  159.1 12.9 %collective-permute-start.9 = (bf16[512,256]{1,0:T(8,128)(2,1)}, bf16[512,256]{1,0:T(8,128)(2,1)S(1)}, u32[]{:S(2)}, u32[]{:S(2)}) collective-permute-start(bf16[512,256]{1,0:T(8,128)(2,1)} %get-tuple-element.30.refs_9_), channel_id=1, source_target_pairs={{0,3},{1,0},{2,1},{3,2},{4,7},{5,4},{6,5},{7,6},{8,11},{9,8},{10,9... | collective-permute-start | bytes 786440 | tf_op jit(solution)/shard_map/ppermute | solution.py:342
  161.1 10.9 %collective-permute-start.8 = (bf16[512,256]{1,0:T(8,128)(2,1)}, bf16[512,256]{1,0:T(8,128)(2,1)S(1)}, u32[]{:S(2)}, u32[]{:S(2)}) collective-permute-start(bf16[512,256]{1,0:T(8,128)(2,1)} %get-tuple-element.31.refs_10_), channel_id=1, source_target_pairs={{0,1},{1,2},{2,3},{3,0},{4,5},{5,6},{6,7},{7,4},{8,9},{9,10},{10,1... | collective-permute-start | bytes 786440 | tf_op jit(solution)/shard_map/ppermute | solution.py:342
  161.2 1.6 copy-start
  162.7 1.0 copy-start.2
  165.7 10.7 %copy-start.1 = (bf16[4,512,512]{2,1,0:T(8,128)(2,1)S(1)}, bf16[4,512,512]{2,1,0:T(8,128)(2,1)}, u32[]{:S(2)}) copy-start(bf16[4,512,512]{2,1,0:T(8,128)(2,1)} %pad_maximum_fusion.refs_0_.refs_2_.refs_4_.refs_6_.refs_8_.refs_1_.refs_7_) | copy-start | bytes 6291460
  168.7 7.7 %collective-permute-start.10 = (bf16[512,256]{1,0:T(8,128)(2,1)S(1)}, bf16[512,256]{1,0:T(8,128)(2,1)S(1)}, u32[]{:S(2)}, u32[]{:S(2)}) collective-permute-start(bf16[512,256]{1,0:T(8,128)(2,1)S(1)} %collective-permute-done.3.refs_2_), channel_id=1, source_target_pairs={{0,1},{1,2},{2,3},{3,0},{4,5},{5,6},{6,7},{7,4},{8,9},{9,10},{10,1... | collective-permute-start | bytes 786440 | tf_op jit(solution)/shard_map/ppermute | solution.py:342
  168.8 7.6 %collective-permute-start.11 = (bf16[512,256]{1,0:T(8,128)(2,1)S(1)}, bf16[512,256]{1,0:T(8,128)(2,1)S(1)}, u32[]{:S(2)}, u32[]{:S(2)}) collective-permute-start(bf16[512,256]{1,0:T(8,128)(2,1)S(1)} %collective-permute-done.4.refs_6_), channel_id=1, source_target_pairs={{0,3},{1,0},{2,1},{3,2},{4,7},{5,4},{6,5},{7,6},{8,11},{9,8},{10,9... | collective-permute-start | bytes 786440 | tf_op jit(solution)/shard_map/ppermute | solution.py:342
  (3 other events, 2.5 us)

commit v3 on v2

--- a/solution.py
+++ b/solution.py
@@ -73,10 +73,10 @@
     lax.fori_loop(0, rounds, one_round, 0)
 
 
-def project_and_sort(me, sends, activations, w_qk, w_value, order, pair):
+def project_and_sort(me, sends, activations, w_qk, w_value, order):
     tokens, width = activations.shape
-    rounds, heads = order.shape[0], PAIR
-    first = PAIR * pair
+    rounds, heads = order.shape[:2]
+    first = 0
     block = (rounds, 1, 2, QUARTERS, 1, tokens // SPAN, QUARTER, HEAD_DIM)
     shape = (rounds, PAIR, 2, QUARTERS, heads // PAIR) + block[5:]
     return pl.pallas_call(
@@ -170,7 +170,7 @@
         grid=(steps,),
         in_specs=[
             pl.BlockSpec(memory_space=pltpu.SMEM),
-            pl.BlockSpec((blocks, 1, sent, rows, columns), lambda i: (0, 0, 0, 0, 0)),
+            pl.BlockSpec((blocks, 1, sent, rows, columns), lambda i: (0, pair, 0, 0, 0)),
         ],
         out_specs=pl.BlockSpec((blocks // steps, sent, rows, columns), lambda i: (i, 0, 0, 0)),
         out_shape=jax.ShapeDtypeStruct((blocks, sent, rows, columns), jnp.bfloat16),
@@ -270,7 +270,7 @@
         in_specs=[
             pl.BlockSpec(memory_space=pltpu.SMEM),
             pl.BlockSpec(sends.shape, lambda h: (0, 0, 0, 0)),
-            pl.BlockSpec(block, lambda h: (0, h, 0, 0, 0, 0, 0, 0)),
+            pl.BlockSpec(block, lambda h: (0, h, 0, 0, pair, 0, 0, 0)),
             pl.BlockSpec(block[:4] + left.shape[1:], lambda h: (0, h, 0, 0, 0, 0, 0)),
             pl.BlockSpec(order.shape, lambda h: (0, 0, 0)),
         ],
@@ -375,13 +375,8 @@
     def send(pieces):
         return lax.all_to_all(pieces, "seq", split_axis=0, concat_axis=0, tiled=True)
 
-    own, arrived = [], []
-    for pair in range(pairs):
-        rows, sent = project_and_sort(
-            me, span_sends, activations, w_qk, w_value, bucket_order, pair
-        )
-        own.append(rows)
-        arrived.append(send(sent.reshape(seq_count, 1, SENT, QUARTER, HEAD_DIM)))
+    own, sent = project_and_sort(me, span_sends, activations, w_qk, w_value, bucket_order)
+    arrived = send(sent.reshape(seq_count, pairs, SENT, QUARTER, HEAD_DIM))
 
     blocks = []
     for shift in range(head_count):
@@ -395,12 +390,12 @@
     table = left_table(of_round[:, my_seq // (2 * QUARTERS) % PAIR])
     left = []
     for pair in range(pairs):
-        pieces = permute(table, arrived[pair], pair)
-        pieces, arrived[-1], weights = lax.optimization_barrier((pieces, arrived[-1], weights))
+        pieces = permute(table, arrived, pair)
+        pieces, arrived, weights = lax.optimization_barrier((pieces, arrived, weights))
         left.append(send(pieces))
 
     def attended(pair, parts):
-        return attend(me, span_sends, own[pair], left[pair], bucket_order, pair, parts)
+        return attend(me, span_sends, own, left[pair], bucket_order, pair, parts)
 
     (mine,) = attended(0, 1)
     terms = from_all_groups(mine)

time: 179 us -> 179 us (level)
  waiting for transfers between devices: 69.6 us -> 80.9 us
  starting transfers between devices: 43.4 us -> 38.4 us
  Pallas kernels: 52.3 us -> 48.6 us
  other arithmetic: 5.35 us -> 3.43 us
    ppermute x12, waiting for transfers between devices: 4.35 us -> 24.6 us  [passed(): lax.ppermute(array, 'head', [(i, (i + by) % count) for i in range(count)])]
    all_to_all x4 -> x3, waiting for transfers between devices: 65.3 us -> 56.3 us  [send(): lax.all_to_all(pieces, 'seq', split_axis=0, concat_axis=0, tiled=True)]
    all_to_all x4 -> x3, starting transfers between devices: 22.2 us -> 17.2 us  [send(): lax.all_to_all(pieces, 'seq', split_axis=0, concat_axis=0, tiled=True)]
    pallas_call x2 -> x1, Pallas kernels: 20.8 us -> 17.1 us  [project_and_sort(): pl.pallas_call(functools.partial(sort_kernel, first), grid=(heads,), in_s...]
    unnamed x22 -> x14, local copies, waits for them, and re-layouts: 5.16 us -> 4.55 us
  transfers between devices with their start and end apart: 16 -> 15, of which waited for: 5 -> 7; matrix products, arithmetic and copies ran while one was open for 4% -> 3% of each run, Pallas kernels for 22% -> 14%
where the time goes in v3:
time: 179 us; the launch traced here: 178 us
  waiting for transfers between devices  80.9 us (45%)
  Pallas kernels  48.6 us (27%)
  starting transfers between devices  38.4 us (21%)
  local copies, waits for them, and re-layouts  6.66 us (4%)
  other arithmetic  3.43 us (2%)
    all_to_all x3, waiting for transfers between devices, send(): lax.all_to_all(pieces, 'seq', split_axis=0, concat_axis=0, tiled=True)  56.3 us
    ppermute x12, waiting for transfers between devices, passed(): lax.ppermute(array, 'head', [(i, (i + by) % count) for i in range(count)])  24.6 us
    ppermute x12, starting transfers between devices, passed(): lax.ppermute(array, 'head', [(i, (i + by) % count) for i in range(count)])  21.3 us
    pallas_call x2, Pallas kernels, attend(): pl.pallas_call(functools.partial(attend_kernel, PAIR * pair), grid=(PAIR,...  17.9 us
    all_to_all x3, starting transfers between devices, send(): lax.all_to_all(pieces, 'seq', split_axis=0, concat_axis=0, tiled=True)  17.2 us
    pallas_call x1, Pallas kernels, project_and_sort(): pl.pallas_call(functools.partial(sort_kernel, first), grid=(heads,), in_s...  17.1 us
    pallas_call x2, Pallas kernels, permute(): pl.pallas_call(functools.partial(permute_kernel, pair), grid=(steps,), in...  8.67 us
    pallas_call x2, Pallas kernels, project_out(): pl.pallas_call(functools.partial(output_kernel, started is not None, [len...  4.93 us
  transfers between devices with their start and end apart: 15, of which 7 were waited for; matrix products, arithmetic and copies ran while one was open for 3% of the time, Pallas kernels for 14%

profile of v3, /device:TPU:0, one launch (start us, length us, event | category | flops | bytes accessed | tf_op | source)
XLA Modules:
  0.0 178.2 jit_solution(7315400896255542066)
XLA Ops:
  0.0 17.1 %shard_map.64 = (bf16[2,2,2,4,2,16,16,128]{7,6,5,4,3,2,1,0:T(8,128)(2,1)}, bf16[2,2,2,4,2,15,16,128]{7,6,5,4,3,2,1,0:T(8,128)(2,1)}) custom-call(s32[1]{0:T(128)} %bitcast.me_ref, s32[2,4,32,32]{3,2,1,0:T(8,128)} %sends_ref.5, bf16[1024,2048]{1,0:T(8,128)(2,1)} %act_ref.1, bf16[2048,512]{1,0:T(8,128)(2,1)} %wq_ref.1, bf16[2048,512]{1,0:T(8,128)(2,1)} %wv_ref.1, ...), custom_call_target="tpu_custom_call" | custom-call | flops 8589934592 | bytes 12582912 | tf_op jit(solution)/shard_map/pallas_call | solution.py:82
  17.1 7.7 %all-to-all-start = ((bf16[32,2,15,16,128]{4,3,2,1,0:T(8,128)(2,1)}), bf16[32,2,15,16,128]{4,3,2,1,0:T(8,128)(2,1)}, u32[]{:S(2)}, u32[]{:S(2)}) async-start(bf16[32,2,15,16,128]{4,3,2,1,0:T(8,128)(2,1)} %bitcast.17), calls=%async_computation | async-start | bytes 7864320 | tf_op jit(solution)/shard_map/all_to_all | solution.py:376
  26.0 1.9 %collective-permute-start = (bf16[512,512]{1,0:T(8,128)(2,1)}, bf16[512,512]{1,0:T(8,128)(2,1)S(1)}, u32[]{:S(2)}, u32[]{:S(2)}) collective-permute-start(bf16[512,512]{1,0:T(8,128)(2,1)} %get-tuple-element.38), channel_id=1, source_target_pairs={{0,1},{1,2},{2,3},{3,0},{4,5},{5,6},{6,7},{7,4},{8,9},{9,10},{10,1... | collective-permute-start | bytes 1572872 | tf_op jit(solution)/shard_map/ppermute | solution.py:342
  27.9 2.1 %collective-permute-start.2 = (bf16[512,512]{1,0:T(8,128)(2,1)}, bf16[512,512]{1,0:T(8,128)(2,1)S(1)}, u32[]{:S(2)}, u32[]{:S(2)}) collective-permute-start(bf16[512,512]{1,0:T(8,128)(2,1)} %get-tuple-element.39), channel_id=1, source_target_pairs={{0,3},{1,0},{2,1},{3,2},{4,7},{5,4},{6,5},{7,6},{8,11},{9,8},{10,9... | collective-permute-start | bytes 1572872 | tf_op jit(solution)/shard_map/ppermute | solution.py:342
  30.1 1.9 %collective-permute-start.1 = (bf16[512,512]{1,0:T(8,128)(2,1)S(1)}, bf16[512,512]{1,0:T(8,128)(2,1)S(1)}, u32[]{:S(2)}, u32[]{:S(2)}) collective-permute-start(bf16[512,512]{1,0:T(8,128)(2,1)S(1)} %get-tuple-element.40), channel_id=1, source_target_pairs={{0,2},{1,3},{2,0},{3,1},{4,6},{5,7},{6,4},{7,5},{8,10},{9,11},{10,... | collective-permute-start | bytes 1572872 | tf_op jit(solution)/shard_map/ppermute | solution.py:342
  34.7 7.9 %collective-permute-done = bf16[512,512]{1,0:T(8,128)(2,1)S(1)} collective-permute-done((bf16[512,512]{1,0:T(8,128)(2,1)}, bf16[512,512]{1,0:T(8,128)(2,1)S(1)}, u32[]{:S(2)}, u32[]{:S(2)}) %collective-permute-start) | collective-permute-done | bytes 524320 | tf_op jit(solution)/shard_map/ppermute | solution.py:342
  42.6 10.6 %collective-permute-done.2 = bf16[512,512]{1,0:T(8,128)(2,1)S(1)} collective-permute-done((bf16[512,512]{1,0:T(8,128)(2,1)}, bf16[512,512]{1,0:T(8,128)(2,1)S(1)}, u32[]{:S(2)}, u32[]{:S(2)}) %collective-permute-start.2) | collective-permute-done | bytes 524320 | tf_op jit(solution)/shard_map/ppermute | solution.py:342
  56.6 18.7 %all-to-all-done.in_ref = bf16[32,2,15,16,128]{4,3,2,1,0:T(8,128)(2,1)} async-done(((bf16[32,2,15,16,128]{4,3,2,1,0:T(8,128)(2,1)}), bf16[32,2,15,16,128]{4,3,2,1,0:T(8,128)(2,1)}, u32[]{:S(2)}, u32[]{:S(2)}) %all-to-all-start) | async-done | bytes 3932192 | tf_op jit(solution)/shard_map/all_to_all | solution.py:376
  75.4 4.3 %shard_map.65 = bf16[32,15,16,128]{3,2,1,0:T(8,128)(2,1)} custom-call(s32[2,480]{1,0:T(2,128)} %min.12.table_ref, bf16[32,2,15,16,128]{4,3,2,1,0:T(8,128)(2,1)} %all-to-all-done.in_ref), custom_call_target="tpu_custom_call" | custom-call | flops 983040 | bytes 3932160 | tf_op jit(solution)/shard_map/pallas_call | solution.py:168
  79.6 4.7 %all-to-all-start.2 = ((bf16[32,15,16,128]{3,2,1,0:T(8,128)(2,1)}), bf16[32,15,16,128]{3,2,1,0:T(8,128)(2,1)}, u32[]{:S(2)}, u32[]{:S(2)}) async-start(bf16[32,15,16,128]{3,2,1,0:T(8,128)(2,1)} %shard_map.65), calls=%async_computation.2 | async-start | bytes 3932160 | tf_op jit(solution)/shard_map/all_to_all | solution.py:376
  84.3 4.4 %shard_map.66 = bf16[32,15,16,128]{3,2,1,0:T(8,128)(2,1)} custom-call(s32[2,480]{1,0:T(2,128)} %min.12.table_ref, bf16[32,2,15,16,128]{4,3,2,1,0:T(8,128)(2,1)} %all-to-all-done.in_ref), custom_call_target="tpu_custom_call" | custom-call | flops 983040 | bytes 3932160 | tf_op jit(solution)/shard_map/pallas_call | solution.py:168
  88.8 24.0 %all-to-all-done.2 = bf16[32,15,16,128]{3,2,1,0:T(8,128)(2,1)} async-done(((bf16[32,15,16,128]{3,2,1,0:T(8,128)(2,1)}), bf16[32,15,16,128]{3,2,1,0:T(8,128)(2,1)}, u32[]{:S(2)}, u32[]{:S(2)}) %all-to-all-start.2) | async-done | bytes 1966112 | tf_op jit(solution)/shard_map/all_to_all | solution.py:376
  112.8 4.7 %all-to-all-start.1 = ((bf16[32,15,16,128]{3,2,1,0:T(8,128)(2,1)}), bf16[32,15,16,128]{3,2,1,0:T(8,128)(2,1)}, u32[]{:S(2)}, u32[]{:S(2)}) async-start(bf16[32,15,16,128]{3,2,1,0:T(8,128)(2,1)} %shard_map.66), calls=%async_computation.1 | async-start | bytes 3932160 | tf_op jit(solution)/shard_map/all_to_all | solution.py:376
  117.5 9.0 %shard_map.67.refs_1_ = bf16[1024,256]{1,0:T(8,128)(2,1)} custom-call(s32[1]{0:T(128)} %bitcast.me_ref, s32[2,4,32,32]{3,2,1,0:T(8,128)} %sends_ref.5, bf16[2,2,2,4,2,16,16,128]{7,6,5,4,3,2,1,0:T(8,128)(2,1)} %get-tuple-element.19.own_ref, bf16[2,2,2,4,15,16,128]{6,5,4,3,2,1,0:T(8,128)(2,1)} %bitcast.8.left_ref, s32[2,4,1024]{2,1,0:T(4,128)} %order_ref.5), custom_call_target="tpu_custom_call" | custom-call | flops 2415919104 | bytes 4194304 | tf_op jit(solution)/shard_map/pallas_call | solution.py:267
  126.5 3.9 %collective-permute-start.7 = (bf16[1024,256]{1,0:T(8,128)(2,1)}, bf16[1024,256]{1,0:T(8,128)(2,1)}, u32[]{:S(2)}, u32[]{:S(2)}) collective-permute-start(bf16[1024,256]{1,0:T(8,128)(2,1)} %shard_map.67.refs_1_), channel_id=1, source_target_pairs={{0,2},{1,3},{2,0},{3,1},{4,6},{5,7},{6,4},{7,5},{8,10},{9,11},{10,... | collective-permute-start | bytes 1572872 | tf_op jit(solution)/shard_map/ppermute | solution.py:342
  132.4 13.5 %all-to-all-done.1 = bf16[32,15,16,128]{3,2,1,0:T(8,128)(2,1)} async-done(((bf16[32,15,16,128]{3,2,1,0:T(8,128)(2,1)}), bf16[32,15,16,128]{3,2,1,0:T(8,128)(2,1)}, u32[]{:S(2)}, u32[]{:S(2)}) %all-to-all-start.1) | async-done | bytes 1966112 | tf_op jit(solution)/shard_map/all_to_all | solution.py:376
  145.9 8.9 %shard_map.68 = (bf16[512,256]{1,0:T(8,128)(2,1)}, bf16[512,256]{1,0:T(8,128)(2,1)}) custom-call(s32[1]{0:T(128)} %bitcast.me_ref, s32[2,4,32,32]{3,2,1,0:T(8,128)} %sends_ref.5, bf16[2,2,2,4,2,16,16,128]{7,6,5,4,3,2,1,0:T(8,128)(2,1)} %get-tuple-element.19.own_ref, bf16[2,2,2,4,15,16,128]{6,5,4,3,2,1,0:T(8,128)(2,1)} %bitcast.9.left_ref, ...), custom_call_target="tpu_custom_call" | custom-call | flops 2415919104 | bytes 4194304 | tf_op jit(solution)/shard_map/pallas_call | solution.py:267
  154.9 1.9 %collective-permute-start.3 = (bf16[512,256]{1,0:T(8,128)(2,1)}, bf16[512,256]{1,0:T(8,128)(2,1)S(1)}, u32[]{:S(2)}, u32[]{:S(2)}) collective-permute-start(bf16[512,256]{1,0:T(8,128)(2,1)} %get-tuple-element.26.refs_9_), channel_id=1, source_target_pairs={{0,1},{1,2},{2,3},{3,0},{4,5},{5,6},{6,7},{7,4},{8,9},{9,10},{10,1... | collective-permute-start | bytes 786440 | tf_op jit(solution)/shard_map/ppermute | solution.py:342
  156.8 2.2 %collective-permute-start.4 = (bf16[512,256]{1,0:T(8,128)(2,1)}, bf16[512,256]{1,0:T(8,128)(2,1)S(1)}, u32[]{:S(2)}, u32[]{:S(2)}) collective-permute-start(bf16[512,256]{1,0:T(8,128)(2,1)} %get-tuple-element.27.refs_10_), channel_id=1, source_target_pairs={{0,3},{1,0},{2,1},{3,2},{4,7},{5,4},{6,5},{7,6},{8,11},{9,8},{10,9... | collective-permute-start | bytes 786440 | tf_op jit(solution)/shard_map/ppermute | solution.py:342
  159.0 2.0 %collective-permute-start.9 = (bf16[512,256]{1,0:T(8,128)(2,1)}, bf16[512,256]{1,0:T(8,128)(2,1)S(1)}, u32[]{:S(2)}, u32[]{:S(2)}) collective-permute-start(bf16[512,256]{1,0:T(8,128)(2,1)} %get-tuple-element.26.refs_9_), channel_id=1, source_target_pairs={{0,3},{1,0},{2,1},{3,2},{4,7},{5,4},{6,5},{7,6},{8,11},{9,8},{10,9... | collective-permute-start | bytes 786440 | tf_op jit(solution)/shard_map/ppermute | solution.py:342
  165.5 3.0 %shard_map.69.refs_0_ = f32[1024,512]{1,0:T(8,128)S(1)} custom-call(bf16[4,512,512]{2,1,0:T(8,128)(2,1)S(1)} %copy-done, bf16[1024,256]{1,0:T(8,128)(2,1)S(1)} %copy-done.2, bf16[4,512,512]{2,1,0:T(8,128)(2,1)S(1)} %copy-done, bf16[1024,256]{1,0:T(8,128)(2,1)} %collective-permute-done.5.refs_3_, bf16[4,512,512]{2,1,0:T(8,128)(2,1)S(1)} %copy-done, ...), custom_call_target="tpu_custom_call" | custom-call | flops 1342177280 | bytes 7077888 | tf_op jit(solution)/shard_map/pallas_call | solution.py:325
  168.6 3.2 %collective-permute-start.11 = (bf16[512,256]{1,0:T(8,128)(2,1)S(1)}, bf16[512,256]{1,0:T(8,128)(2,1)S(1)}, u32[]{:S(2)}, u32[]{:S(2)}) collective-permute-start(bf16[512,256]{1,0:T(8,128)(2,1)S(1)} %collective-permute-done.4.refs_6_), channel_id=1, source_target_pairs={{0,3},{1,0},{2,1},{3,2},{4,7},{5,4},{6,5},{7,6},{8,11},{9,8},{10,9... | collective-permute-start | bytes 786440 | tf_op jit(solution)/shard_map/ppermute | solution.py:342
  171.9 4.3 %collective-permute-done.10.refs_8_ = bf16[512,256]{1,0:T(8,128)(2,1)S(1)} collective-permute-done((bf16[512,256]{1,0:T(8,128)(2,1)S(1)}, bf16[512,256]{1,0:T(8,128)(2,1)S(1)}, u32[]{:S(2)}, u32[]{:S(2)}) %collective-permute-start.10) | collective-permute-done | bytes 262176 | tf_op jit(solution)/shard_map/ppermute | solution.py:342
  176.2 2.0 %shard_map.70 = bf16[1024,512]{1,0:T(8,128)(2,1)} custom-call(f32[1024,512]{1,0:T(8,128)S(1)} %shard_map.69.refs_0_, bf16[4,512,512]{2,1,0:T(8,128)(2,1)S(1)} %copy-done.1, bf16[512,256]{1,0:T(8,128)(2,1)S(1)} %collective-permute-done.3.refs_2_, bf16[512,256]{1,0:T(8,128)(2,1)S(1)} %collective-permute-done.8.refs_3_, bf16[4,512,512]{2,1,0:T(8,128)(2,1)S(1)} %copy-done.1, ...), custom_call_target="tpu_custom_call" | custom-call | flops 805306368 | bytes 5505024 | tf_op jit(solution)/shard_map/pallas_call | solution.py:325
  (46 shorter events, 14.1 us)
Async XLA Ops:
  17.1 7.7 %copy-start.5 = (bf16[512,2048]{1,0:T(8,128)(2,1)S(1)}, bf16[512,2048]{1,0:T(8,128)(2,1)}, u32[]{:S(2)}) copy-start(bf16[512,2048]{1,0:T(8,128)(2,1)} %param.9) | copy-start | bytes 6291460
  17.1 58.3 %all-to-all-start = ((bf16[32,2,15,16,128]{4,3,2,1,0:T(8,128)(2,1)}), bf16[32,2,15,16,128]{4,3,2,1,0:T(8,128)(2,1)}, u32[]{:S(2)}, u32[]{:S(2)}) async-start(bf16[32,2,15,16,128]{4,3,2,1,0:T(8,128)(2,1)} %bitcast.17), calls=%async_computation | async-start | bytes 7864320 | tf_op jit(solution)/shard_map/all_to_all | solution.py:376
  24.8 7.2 %copy-start.6 = (s32[2,4,32,32]{3,2,1,0:T(8,128)S(1)}, s32[2,4,32,32]{3,2,1,0:T(8,128)}, u32[]{:S(2)}) copy-start(s32[2,4,32,32]{3,2,1,0:T(8,128)} %sends_ref.5) | copy-start | bytes 98308
  26.0 16.5 %collective-permute-start = (bf16[512,512]{1,0:T(8,128)(2,1)}, bf16[512,512]{1,0:T(8,128)(2,1)S(1)}, u32[]{:S(2)}, u32[]{:S(2)}) collective-permute-start(bf16[512,512]{1,0:T(8,128)(2,1)} %get-tuple-element.38), channel_id=1, source_target_pairs={{0,1},{1,2},{2,3},{3,0},{4,5},{5,6},{6,7},{7,4},{8,9},{9,10},{10,1... | collective-permute-start | bytes 1572872 | tf_op jit(solution)/shard_map/ppermute | solution.py:342
  27.9 25.3 %collective-permute-start.2 = (bf16[512,512]{1,0:T(8,128)(2,1)}, bf16[512,512]{1,0:T(8,128)(2,1)S(1)}, u32[]{:S(2)}, u32[]{:S(2)}) collective-permute-start(bf16[512,512]{1,0:T(8,128)(2,1)} %get-tuple-element.39), channel_id=1, source_target_pairs={{0,3},{1,0},{2,1},{3,2},{4,7},{5,4},{6,5},{7,6},{8,11},{9,8},{10,9... | collective-permute-start | bytes 1572872 | tf_op jit(solution)/shard_map/ppermute | solution.py:342
  30.1 24.9 %collective-permute-start.1 = (bf16[512,512]{1,0:T(8,128)(2,1)S(1)}, bf16[512,512]{1,0:T(8,128)(2,1)S(1)}, u32[]{:S(2)}, u32[]{:S(2)}) collective-permute-start(bf16[512,512]{1,0:T(8,128)(2,1)S(1)} %get-tuple-element.40), channel_id=1, source_target_pairs={{0,2},{1,3},{2,0},{3,1},{4,6},{5,7},{6,4},{7,5},{8,10},{9,11},{10,... | collective-permute-start | bytes 1572872 | tf_op jit(solution)/shard_map/ppermute | solution.py:342
  79.6 33.2 %all-to-all-start.2 = ((bf16[32,15,16,128]{3,2,1,0:T(8,128)(2,1)}), bf16[32,15,16,128]{3,2,1,0:T(8,128)(2,1)}, u32[]{:S(2)}, u32[]{:S(2)}) async-start(bf16[32,15,16,128]{3,2,1,0:T(8,128)(2,1)} %shard_map.65), calls=%async_computation.2 | async-start | bytes 3932160 | tf_op jit(solution)/shard_map/all_to_all | solution.py:376
  112.8 33.2 %all-to-all-start.1 = ((bf16[32,15,16,128]{3,2,1,0:T(8,128)(2,1)}), bf16[32,15,16,128]{3,2,1,0:T(8,128)(2,1)}, u32[]{:S(2)}, u32[]{:S(2)}) async-start(bf16[32,15,16,128]{3,2,1,0:T(8,128)(2,1)} %shard_map.66), calls=%async_computation.1 | async-start | bytes 3932160 | tf_op jit(solution)/shard_map/all_to_all | solution.py:376
  126.5 32.5 %collective-permute-start.7 = (bf16[1024,256]{1,0:T(8,128)(2,1)}, bf16[1024,256]{1,0:T(8,128)(2,1)}, u32[]{:S(2)}, u32[]{:S(2)}) collective-permute-start(bf16[1024,256]{1,0:T(8,128)(2,1)} %shard_map.67.refs_1_), channel_id=1, source_target_pairs={{0,2},{1,3},{2,0},{3,1},{4,6},{5,7},{6,4},{7,5},{8,10},{9,11},{10,... | collective-permute-start | bytes 1572872 | tf_op jit(solution)/shard_map/ppermute | solution.py:342
  130.4 30.6 %collective-permute-start.6 = (bf16[1024,256]{1,0:T(8,128)(2,1)}, bf16[1024,256]{1,0:T(8,128)(2,1)}, u32[]{:S(2)}, u32[]{:S(2)}) collective-permute-start(bf16[1024,256]{1,0:T(8,128)(2,1)} %shard_map.67.refs_1_), channel_id=1, source_target_pairs={{0,3},{1,0},{2,1},{3,2},{4,7},{5,4},{6,5},{7,6},{8,11},{9,8},{10,9... | collective-permute-start | bytes 1572872 | tf_op jit(solution)/shard_map/ppermute | solution.py:342
  131.1 29.9 %collective-permute-start.5 = (bf16[1024,256]{1,0:T(8,128)(2,1)}, bf16[1024,256]{1,0:T(8,128)(2,1)}, u32[]{:S(2)}, u32[]{:S(2)}) collective-permute-start(bf16[1024,256]{1,0:T(8,128)(2,1)} %shard_map.67.refs_1_), channel_id=1, source_target_pairs={{0,1},{1,2},{2,3},{3,0},{4,5},{5,6},{6,7},{7,4},{8,9},{9,10},{10,1... | collective-permute-start | bytes 1572872 | tf_op jit(solution)/shard_map/ppermute | solution.py:342
  154.9 13.7 %collective-permute-start.3 = (bf16[512,256]{1,0:T(8,128)(2,1)}, bf16[512,256]{1,0:T(8,128)(2,1)S(1)}, u32[]{:S(2)}, u32[]{:S(2)}) collective-permute-start(bf16[512,256]{1,0:T(8,128)(2,1)} %get-tuple-element.26.refs_9_), channel_id=1, source_target_pairs={{0,1},{1,2},{2,3},{3,0},{4,5},{5,6},{6,7},{7,4},{8,9},{9,10},{10,1... | collective-permute-start | bytes 786440 | tf_op jit(solution)/shard_map/ppermute | solution.py:342
  156.8 11.8 %collective-permute-start.4 = (bf16[512,256]{1,0:T(8,128)(2,1)}, bf16[512,256]{1,0:T(8,128)(2,1)S(1)}, u32[]{:S(2)}, u32[]{:S(2)}) collective-permute-start(bf16[512,256]{1,0:T(8,128)(2,1)} %get-tuple-element.27.refs_10_), channel_id=1, source_target_pairs={{0,3},{1,0},{2,1},{3,2},{4,7},{5,4},{6,5},{7,6},{8,11},{9,8},{10,9... | collective-permute-start | bytes 786440 | tf_op jit(solution)/shard_map/ppermute | solution.py:342
  159.0 12.9 %collective-permute-start.9 = (bf16[512,256]{1,0:T(8,128)(2,1)}, bf16[512,256]{1,0:T(8,128)(2,1)S(1)}, u32[]{:S(2)}, u32[]{:S(2)}) collective-permute-start(bf16[512,256]{1,0:T(8,128)(2,1)} %get-tuple-element.26.refs_9_), channel_id=1, source_target_pairs={{0,3},{1,0},{2,1},{3,2},{4,7},{5,4},{6,5},{7,6},{8,11},{9,8},{10,9... | collective-permute-start | bytes 786440 | tf_op jit(solution)/shard_map/ppermute | solution.py:342
  160.9 10.9 %collective-permute-start.8 = (bf16[512,256]{1,0:T(8,128)(2,1)}, bf16[512,256]{1,0:T(8,128)(2,1)S(1)}, u32[]{:S(2)}, u32[]{:S(2)}) collective-permute-start(bf16[512,256]{1,0:T(8,128)(2,1)} %get-tuple-element.27.refs_10_), channel_id=1, source_target_pairs={{0,1},{1,2},{2,3},{3,0},{4,5},{5,6},{6,7},{7,4},{8,9},{9,10},{10,1... | collective-permute-start | bytes 786440 | tf_op jit(solution)/shard_map/ppermute | solution.py:342
  161.0 1.6 copy-start
  162.6 1.0 copy-start.2
  163.6 0.9 copy-start.3
  164.6 0.9 copy-start.4
  165.5 10.7 %copy-start.1 = (bf16[4,512,512]{2,1,0:T(8,128)(2,1)S(1)}, bf16[4,512,512]{2,1,0:T(8,128)(2,1)}, u32[]{:S(2)}) copy-start(bf16[4,512,512]{2,1,0:T(8,128)(2,1)} %pad_maximum_fusion.refs_0_.refs_2_.refs_4_.refs_6_.refs_8_.refs_1_.refs_7_) | copy-start | bytes 6291460
  168.5 7.7 %collective-permute-start.10 = (bf16[512,256]{1,0:T(8,128)(2,1)S(1)}, bf16[512,256]{1,0:T(8,128)(2,1)S(1)}, u32[]{:S(2)}, u32[]{:S(2)}) collective-permute-start(bf16[512,256]{1,0:T(8,128)(2,1)S(1)} %collective-permute-done.3.refs_2_), channel_id=1, source_target_pairs={{0,1},{1,2},{2,3},{3,0},{4,5},{5,6},{6,7},{7,4},{8,9},{9,10},{10,1... | collective-permute-start | bytes 786440 | tf_op jit(solution)/shard_map/ppermute | solution.py:342
  168.6 7.6 %collective-permute-start.11 = (bf16[512,256]{1,0:T(8,128)(2,1)S(1)}, bf16[512,256]{1,0:T(8,128)(2,1)S(1)}, u32[]{:S(2)}, u32[]{:S(2)}) collective-permute-start(bf16[512,256]{1,0:T(8,128)(2,1)S(1)} %collective-permute-done.4.refs_6_), channel_id=1, source_target_pairs={{0,3},{1,0},{2,1},{3,2},{4,7},{5,4},{6,5},{7,6},{8,11},{9,8},{10,9... | collective-permute-start | bytes 786440 | tf_op jit(solution)/shard_map/ppermute | solution.py:342
